TPU v7x, 512 devices: a whole 4x4x16 slice. The times are simulated.
512 devices in a mesh: gx: 16 (over x, y), gy: 32 (over z, core).
Axes of the slice: x: 4, y: 4, z: 16, core: 2. Of those that a mesh axis runs over, the one named last changes fastest.
Arguments:
- features: bfloat16 [1703936, 512], P(('gx', 'gy')), may hold values from -16 to 16
- sketch: bfloat16 [512, 64], replicated, may hold values from -6 to 6
Outputs:
- basis: float32 [512, 64], replicated
- codes: bfloat16 [1703936, 64], P(('gx', 'gy'))
- left_factor: float32 [1703936, 64], P(('gx', 'gy'))
All inputs are finite; a program needn't handle non-finite values.
Results may differ from a plain program's by a relative error of at most 0.0065.
Values sent between devices are 32-bit elements; how exact they have to be, the bound alone decides.
No kernel may reach another device: no remote copies, remote signals or barrier semaphores. Data moves between devices by JAX's collectives and lax.ppermute only.
A program may use at most 64 MiB of HBM per device.

v0:
```python
import math

import jax
import jax.numpy as jnp
from jax import lax
from jax.sharding import PartitionSpec as P


def left_product(features, tall):
    upper = tall.astype(jnp.bfloat16)
    lower = (tall - upper.astype(jnp.float32)).astype(jnp.bfloat16)
    dims = (((0,), (0,)), ((), ()))
    return lax.dot_general(
        features, upper, dims, preferred_element_type=jnp.float32
    ) + lax.dot_general(features, lower, dims, preferred_element_type=jnp.float32)


def solve_right(factor, matrix):
    return lax.linalg.triangular_solve(
        factor, matrix, left_side=False, lower=True, transpose_a=True
    )


def orthonormal(matrix):
    for sweep in range(2):
        gram = jnp.dot(matrix.T, matrix, precision=lax.Precision.HIGHEST)
        matrix = solve_right(jnp.linalg.cholesky(gram), matrix)
    return matrix


def on_device(features, sketch):
    scale = math.sqrt(features.shape[0] * lax.axis_size("gx") * lax.axis_size("gy"))
    first = jnp.dot(features, sketch, preferred_element_type=jnp.float32)
    wide = lax.psum(left_product(features, first), ("gx", "gy"))
    estimate = orthonormal(wide).astype(jnp.bfloat16)
    second = jnp.dot(features, estimate, preferred_element_type=jnp.float32)
    gram = lax.psum(jnp.dot(second.T, second, precision=lax.Precision.HIGHEST), ("gx", "gy"))
    tall = solve_right(jnp.linalg.cholesky(gram), second)
    partial_sum = left_product(features, tall)
    projected = lax.psum(partial_sum, ("gx", "gy"))
    basis = orthonormal(projected)
    left_factor = tall * scale
    codes = jnp.dot(
        features, basis.astype(jnp.bfloat16), preferred_element_type=jnp.float32
    ).astype(jnp.bfloat16)
    return (basis, codes, left_factor)


def solution(mesh):
    placed = (P(("gx", "gy"), None), P())
    return jax.shard_map(
        on_device,
        mesh=mesh,
        in_specs=placed,
        out_specs=(P(), P(("gx", "gy"), None), P(("gx", "gy"), None)),
        check_vma=False,
    )
```

profile of v0, /device:TPU:1, one launch (start us, length us, event | category | flops | bytes accessed | tf_op | source)
XLA Modules:
  0.0 1109.2 jit_solution(2047056601737940968)
XLA Ops:
  7.2 0.0 copy-start
  7.2 0.0 all-reduce.3.cloned.1.call-start
  7.2 1.9 copy-done
  9.1 2.0 fusion.35
  11.1 0.7 fusion.8
  11.8 1.4 fusion.2
  13.2 0.0 all-reduce.3.cloned.1.call-update
  13.2 0.0 all-reduce.5.cloned.1.call-start
  13.3 454.0 %all-reduce.3.cloned.1.call-done = f32[512,64]{0,1:T(8,128)} async-done(((f32[512,64]{0,1:T(8,128)}), f32[512,64]{0,1:T(8,128)}) %all-reduce.3.cloned.1.call-update) | async-done | bytes 131088 | tf_op jit(solution)/shard_map/psum | solution.py:34
  467.2 1.2 fusion.36
  468.5 0.1 copy.5
  468.6 5.8 cholesky.89
  474.4 0.6 compare_reduce_fusion.4
  475.1 0.7 fusion.11
  475.7 5.5 custom-call.12
  481.3 1.2 convolution_bitcast_fusion.3
  482.5 0.9 fusion.37
  483.4 1.5 copy.6
  484.8 1.4 fusion.24
  486.2 7.2 cholesky.100
  493.5 0.8 fusion.32
  494.3 0.6 compare_reduce_fusion.3
  494.9 2.0 fusion.12
  496.9 6.3 custom-call.13
  503.2 1.1 fusion.3
  504.3 1.1 fusion.38
  505.4 0.0 copy-start.1
  505.4 0.9 copy-done.1
  506.3 0.8 fusion.39
  507.2 100.1 %psum.22 = f32[64,64]{0,1:T(8,128)S(1)} all-reduce(f32[64,64]{0,1:T(8,128)S(1)} %fusion.39), channel_id=1, replica_groups=mesh['gx'=16,'gy'=32] {'gx','gy'}, use_global_device_ids=true, to_apply=%region_3.6 | all-reduce | flops 4096 | bytes 32768 | tf_op jit(solution)/shard_map/psum | solution.py:37
  607.2 0.1 copy.8
  607.3 5.8 cholesky.111
  613.2 0.6 compare_reduce_fusion.2
  613.8 0.7 fusion.13
  614.5 4.9 custom-call.8
  619.4 2.9 broadcast_multiply_fusion
  622.3 0.7 fusion.5
  623.0 1.4 fusion.1
  624.4 0.0 all-reduce.5.cloned.1.call-update
  624.4 438.9 %all-reduce.5.cloned.1.call-done = f32[512,64]{0,1:T(8,128)} async-done(((f32[512,64]{0,1:T(8,128)}), f32[512,64]{0,1:T(8,128)}) %all-reduce.5.cloned.1.call-update) | async-done | bytes 131088 | tf_op jit(solution)/shard_map/psum | solution.py:40
  1063.4 1.2 fusion.40
  1064.6 0.1 copy.9
  1064.7 5.8 cholesky.122
  1070.6 0.6 compare_reduce_fusion.1
  1071.2 0.7 fusion.14
  1071.9 5.5 custom-call.14
  1077.4 1.2 convolution_bitcast_fusion.1
  1078.7 0.9 fusion.41
  1079.5 1.5 copy.10
  1081.0 1.4 fusion.17
  1082.4 7.2 cholesky.133
  1089.6 0.8 select_reduce_fusion
  1090.4 0.6 compare_reduce_fusion
  1091.0 2.0 fusion.15
  1093.1 6.3 custom-call.15
  1099.4 1.1 convolution_bitcast_fusion
  1100.4 0.0 copy-start.2
  1100.4 1.9 fusion
  1102.3 0.0 copy-done.2
  (6 shorter events, 0.1 us)
Async XLA Ops:
  7.2 2.0 copy-start
  7.2 460.0 %all-reduce.3.cloned.1.call-start = ((), (), s32[]{:S(2)}) async-start(), calls=%async_computation | async-start | bytes 262144 | tf_op jit(solution)/shard_map/psum | solution.py:34
  13.2 1050.2 %all-reduce.5.cloned.1.call-start = ((), (), s32[]{:S(2)}) async-start(), calls=%async_computation.1 | async-start | bytes 262144 | tf_op jit(solution)/shard_map/psum | solution.py:40
  505.4 0.9 copy-start.1
  1100.4 1.9 copy-start.2
Sparse Core Ops, SparseCore 0:
  14.0 453.1 all-reduce.2
  624.6 438.7 all-reduce.4
where the time goes:
time: 1110 us
  waiting for transfers between devices  893 us (80%)
  blocking collectives  100 us (9%)
  other arithmetic  74.2 us (7%)
  matrix products  21.7 us (2%)
  between operations  14.2 us (1%)
    psum x1, waiting for transfers between devices, on_device(): wide = lax.psum(left_product(features, first), ('gx', 'gy'))  454 us
    psum x1, waiting for transfers between devices, on_device(): projected = lax.psum(partial_sum, ('gx', 'gy'))  439 us
    psum x1, blocking collectives, on_device(): lax.psum(jnp.dot(second.T, second, precision=lax.Precision.HIGHEST), ('gx...  100 us
    another operation x10, other arithmetic, solve_right(): lax.linalg.triangular_solve(factor, matrix, left_side=False, lower=True,...  34.5 us
    another operation x12, other arithmetic, orthonormal(): matrix = solve_right(jnp.linalg.cholesky(gram), matrix)  30.3 us
  transfers between devices with their start and end apart: 2, of which 2 were waited for; matrix products, arithmetic and copies ran while one was open for 0% of the time, Pallas kernels for 0%

commit v1 on v0

v1 whole, which is shorter than its diff:
```python
import math

import jax
import jax.numpy as jnp
from jax import lax
from jax.sharding import Mesh, PartitionSpec as P

BLOCK = 128
HIGHEST = lax.Precision.HIGHEST


def solve_right(factor, matrix):
    return lax.linalg.triangular_solve(
        factor, matrix, left_side=False, lower=True, transpose_a=True
    )


def sweep(matrix):
    gram = jnp.dot(matrix.T, matrix, precision=HIGHEST)
    return solve_right(jnp.linalg.cholesky(gram), matrix)


def orthonormal(matrix):
    return sweep(sweep(matrix))


def exchange(parts, axes):
    return lax.all_to_all(parts, axes, split_axis=0, concat_axis=0, tiled=True)


def pack(gram):
    n = gram.shape[0] // BLOCK
    cut = lambda i, j: gram[i * BLOCK : (i + 1) * BLOCK, j * BLOCK : (j + 1) * BLOCK]
    return jnp.concatenate([cut(i, j) for i in range(n) for j in range(i, n)], axis=0)


def unpack(packed, n):
    blocks = {}
    at = 0
    for i in range(n):
        for j in range(i, n):
            blocks[i, j] = packed[at : at + BLOCK]
            at += BLOCK
    rows = []
    for i in range(n):
        row = [blocks[i, j] if j >= i else blocks[j, i].T for j in range(n)]
        rows.append(jnp.concatenate(row, axis=1))
    return jnp.concatenate(rows, axis=0)


def sum_everywhere(packed):
    plane = lax.axis_size(("gx", "c"))
    rows, width = packed.shape
    share = jnp.sum(exchange(packed.reshape(plane, rows // plane, width), ("gx", "c")), axis=0)
    line = lax.axis_size("z")
    share = jnp.sum(exchange(jnp.broadcast_to(share, (line, *share.shape)), "z"), axis=0)
    whole = exchange(jnp.broadcast_to(share, (plane, *share.shape)), ("gx", "c"))
    return whole.reshape(rows, width)


def on_device(features, sketch):
    width = features.shape[1]
    scale = math.sqrt(features.shape[0] * lax.axis_size(("gx", "z", "c")))
    local = lax.dot_general(
        features, features, (((0,), (0,)), ((), ())), preferred_element_type=jnp.float32
    )
    gram = unpack(sum_everywhere(pack(local)), width // BLOCK)
    wide = jnp.dot(gram, sketch.astype(jnp.float32), precision=HIGHEST)
    estimate = orthonormal(wide).astype(jnp.bfloat16)
    near = estimate.astype(jnp.float32)
    image = jnp.dot(gram, near, precision=HIGHEST)
    factor = jnp.linalg.cholesky(jnp.dot(near.T, image, precision=HIGHEST))
    basis = orthonormal(solve_right(factor, image))
    second = jnp.dot(features, estimate, preferred_element_type=jnp.float32)
    left_factor = solve_right(factor, second) * scale
    codes = jnp.dot(
        features, basis.astype(jnp.bfloat16), preferred_element_type=jnp.float32
    ).astype(jnp.bfloat16)
    return (basis, codes, left_factor)


def solution(mesh):
    rows, columns = mesh.devices.shape
    mesh = Mesh(mesh.devices.reshape(rows, columns // 2, 2), ("gx", "z", "c"))
    split = P(("gx", "z", "c"), None)
    return jax.shard_map(
        on_device,
        mesh=mesh,
        in_specs=(split, P()),
        out_specs=(P(), split, split),
        check_vma=False,
    )
```

time: 1110 us -> 202 us (0.18)
  waiting for transfers between devices: 893 us -> 0 us
  blocking collectives: 100 us -> 74.3 us
  between operations: 14.2 us -> 0.91 us
  local copies, waits for them, and re-layouts: 5.96 us -> 18.9 us
  other arithmetic: 74.2 us -> 85.5 us
    psum x2 -> x0, waiting for transfers between devices: 893 us -> none  [the longest x1 454 us: on_device(): wide = lax.psum(left_product(features, first), ('gx', 'gy'))]
    psum x1 -> x0, blocking collectives: 100 us -> none  [on_device(): lax.psum(jnp.dot(second.T, second, precision=lax.Precision.HIGHEST), ('gx...]
    all_to_all x0 -> x3, blocking collectives: none -> 74.3 us  [exchange(): return lax.all_to_all(parts, axes, split_axis=0, concat_axis=0, tiled=True)]
  transfers between devices with their start and end apart: 2 -> 0, of which waited for: 2 -> 0; matrix products, arithmetic and copies ran while one was open for 0% -> 0% of each run, Pallas kernels for 0% -> 0%
where the time goes in v1:
time: 202 us; the launch traced here: 200 us
  other arithmetic  85.5 us (42%)
  blocking collectives  74.3 us (37%)
  matrix products  19.9 us (10%)
  local copies, waits for them, and re-layouts  18.9 us (9%)
    all_to_all x3, blocking collectives, exchange(): return lax.all_to_all(parts, axes, split_axis=0, concat_axis=0, tiled=True)  74.3 us
    another operation x10, other arithmetic, solve_right(): lax.linalg.triangular_solve(factor, matrix, left_side=False, lower=True,...  37.3 us
    another operation x12, other arithmetic, sweep(): return solve_right(jnp.linalg.cholesky(gram), matrix)  30.3 us
    another operation x3, other arithmetic, on_device(): factor = jnp.linalg.cholesky(jnp.dot(near.T, image, precision=HIGHEST))  8.65 us
    another operation x6, matrix products, solve_right(): lax.linalg.triangular_solve(factor, matrix, left_side=False, lower=True,...  7.55 us
    unnamed x25, local copies, waits for them, and re-layouts  6.92 us
    transpose x3, local copies, waits for them, and re-layouts, unpack(): row = [blocks[i, j] if j >= i else blocks[j, i].T for j in range(n)]  4.67 us

profile of v1, /device:TPU:1, one launch (start us, length us, event | category | flops | bytes accessed | tf_op | source)
XLA Modules:
  0.0 199.5 jit_solution(9385039429088987726)
XLA Ops:
  0.6 2.0 copy-done
  2.6 1.9 fusion.28
  4.7 23.2 %all_to_all.15 = f32[32,40,128]{2,1,0:T(8,128)} all-to-all(f32[32,40,128]{2,1,0:T(8,128)S(1)} %bitcast.101), channel_id=1, replica_groups=mesh['gx'=16,'z'=16,'c'=2] {'gx','c'}, dimensions={0} | all-to-all | bytes 1310720 | tf_op jit(solution)/shard_map/all_to_all | solution.py:28
  28.0 1.1 reduce_sum.18
  29.1 31.2 %all_to_all.16 = f32[16,40,128]{2,1,0:T(8,128)} all-to-all(f32[16,40,128]{2,1,0:T(8,128)S(1)} %broadcast_in_dim.7), channel_id=1, replica_groups=mesh['gx'=16,'z'=16,'c'=2] {'z'}, dimensions={0} | all-to-all | bytes 655360 | tf_op jit(solution)/shard_map/all_to_all | solution.py:28
  60.3 1.0 reduce_sum.19
  61.4 19.9 %all_to_all.17 = f32[32,40,128]{2,1,0:T(8,128)S(1)} all-to-all(f32[32,40,128]{2,1,0:T(8,128)S(1)} %broadcast_in_dim.8), channel_id=1, replica_groups=mesh['gx'=16,'z'=16,'c'=2] {'gx','c'}, dimensions={0} | all-to-all | bytes 1310720 | tf_op jit(solution)/shard_map/all_to_all | solution.py:28
  81.3 0.9 fusion.27
  82.2 0.1 copy.30
  82.2 0.9 copy.31
  83.2 1.6 copy.20
  84.8 1.6 copy.21
  86.3 1.6 copy.22
  87.9 1.6 copy.29
  89.4 1.6 pad_maximum_fusion
  91.0 1.8 copy.23
  92.8 1.3 maximum_maximum_fusion
  94.1 1.0 copy-done.1
  95.1 1.5 fusion.29
  96.6 0.6 copy-done.4
  97.3 0.3 fusion.30
  97.6 5.8 %cholesky.89 = f32[64,64]{1,0:T(8,128)S(1)} custom-call(f32[64,64]{1,0:T(8,128)S(1)} %fusion.18), custom_call_target="Cholesky" | custom-call | tf_op jit(solution)/shard_map/jit(cholesky)/cholesky | solution.py:20
  103.5 0.6 compare_reduce_fusion.4
  104.1 0.7 fusion.3
  104.8 5.5 %custom-call.13 = f32[1,64,64]{1,2,0:T(8,128)} custom-call(f32[1,64,64]{2,1,0:T(8,128)S(1)} %fusion.3), custom_call_target="InvertDiagBlocksLowerTriangular" | custom-call | tf_op jit(solution)/shard_map/triangular_solve/custom-call.0 | solution.py:13
  110.3 1.2 convolution_bitcast_fusion.4
  111.6 0.9 fusion.31
  112.4 1.5 copy.25
  113.9 1.4 fusion.16
  115.3 7.2 %cholesky.100 = f32[64,64]{1,0:T(8,128)} custom-call(f32[64,64]{1,0:T(8,128)} %fusion.16), custom_call_target="Cholesky" | custom-call | tf_op jit(solution)/shard_map/jit(cholesky)/cholesky | solution.py:20
  122.5 0.8 fusion.25
  123.3 0.6 compare_reduce_fusion.3
  123.9 2.0 %fusion.4 = f32[1,64,64]{2,1,0:T(8,128)} fusion(f32[64,64]{1,0:T(8,128)} %cholesky.100, pred[]{:T(512)} %compare_reduce_fusion.3), kind=kLoop, calls=%fused_computation.27 | loop fusion | flops 16384 | bytes 32769 | tf_op jit(solution)/shard_map/triangular_solve/reshape.13 | solution.py:13
  126.0 6.3 %custom-call.14 = f32[1,64,64]{1,2,0:T(8,128)} custom-call(f32[1,64,64]{2,1,0:T(8,128)} %fusion.4), custom_call_target="InvertDiagBlocksLowerTriangular" | custom-call | tf_op jit(solution)/shard_map/triangular_solve/custom-call.0 | solution.py:13
  132.3 1.1 fusion.1
  133.3 1.9 fusion.32
  135.2 2.1 %fusion.36 = f32[64,3328]{1,0:T(8,128)} fusion(bf16[512,64]{0,1:T(8,128)(2,1)S(1)} %fusion.1, bf16[3328,512]{1,0:T(8,128)(2,1)S(1)} %copy-done), kind=kOutput, calls=%fused_computation.76 | convolution fusion | flops 218103808 | bytes 4325376 | tf_op jit(solution)/shard_map/dot_general | solution.py:74
  137.3 0.8 fusion.33
  138.1 1.5 copy.26
  139.6 1.4 fusion.14
  141.0 7.2 %cholesky.111 = f32[64,64]{1,0:T(8,128)} custom-call(f32[64,64]{1,0:T(8,128)} %fusion.14), custom_call_target="Cholesky" | custom-call | tf_op jit(solution)/shard_map/jit(cholesky)/cholesky | solution.py:72
  148.2 0.8 fusion.24
  149.0 0.6 compare_reduce_fusion.2
  149.6 2.0 %fusion.5 = f32[1,64,64]{2,1,0:T(8,128)} fusion(f32[64,64]{1,0:T(8,128)} %cholesky.111, pred[]{:T(512)} %compare_reduce_fusion.2), kind=kLoop, calls=%fused_computation.28 | loop fusion | flops 16384 | bytes 32769 | tf_op jit(solution)/shard_map/triangular_solve/reshape.13 | solution.py:13
  151.6 6.3 %custom-call.15 = f32[1,64,64]{1,2,0:T(8,128)} custom-call(f32[1,64,64]{2,1,0:T(8,128)} %fusion.5), custom_call_target="InvertDiagBlocksLowerTriangular" | custom-call | tf_op jit(solution)/shard_map/triangular_solve/custom-call.0 | solution.py:13
  157.9 1.1 convolution_bitcast_fusion.2
  159.0 0.6 copy-done.3
  159.6 0.3 fusion.34
  160.0 5.8 %cholesky.122 = f32[64,64]{1,0:T(8,128)S(1)} custom-call(f32[64,64]{1,0:T(8,128)S(1)} %fusion.11), custom_call_target="Cholesky" | custom-call | tf_op jit(solution)/shard_map/jit(cholesky)/cholesky | solution.py:20
  165.9 0.6 compare_reduce_fusion.1
  166.5 0.7 fusion.6
  167.2 5.5 %custom-call.16 = f32[1,64,64]{1,2,0:T(8,128)} custom-call(f32[1,64,64]{2,1,0:T(8,128)S(1)} %fusion.6), custom_call_target="InvertDiagBlocksLowerTriangular" | custom-call | tf_op jit(solution)/shard_map/triangular_solve/custom-call.0 | solution.py:13
  172.7 1.2 convolution_bitcast_fusion.1
  174.0 0.9 fusion.35
  174.8 1.5 copy.28
  176.3 1.4 fusion.9
  177.7 7.2 %cholesky.133 = f32[64,64]{1,0:T(8,128)} custom-call(f32[64,64]{1,0:T(8,128)} %fusion.9), custom_call_target="Cholesky" | custom-call | tf_op jit(solution)/shard_map/jit(cholesky)/cholesky | solution.py:20
  184.9 0.8 select_reduce_fusion
  185.7 0.6 compare_reduce_fusion
  186.3 2.0 %fusion.7 = f32[1,64,64]{2,1,0:T(8,128)} fusion(f32[64,64]{1,0:T(8,128)} %cholesky.133, pred[]{:T(512)} %compare_reduce_fusion), kind=kLoop, calls=%fused_computation.30 | loop fusion | flops 16384 | bytes 32769 | tf_op jit(solution)/shard_map/triangular_solve/reshape.13 | solution.py:13
  188.4 6.3 %custom-call.17 = f32[1,64,64]{1,2,0:T(8,128)} custom-call(f32[1,64,64]{2,1,0:T(8,128)} %fusion.7), custom_call_target="InvertDiagBlocksLowerTriangular" | custom-call | tf_op jit(solution)/shard_map/triangular_solve/custom-call.0 | solution.py:13
  194.7 1.1 convolution_bitcast_fusion
  195.8 1.9 fusion
  197.7 1.8 convolution_multiply_fusion
  (27 shorter events, 0.4 us)
Async XLA Ops:
  0.6 2.0 copy-start
  94.1 1.0 copy-start.1
  96.6 0.7 copy-start.4
  159.0 0.7 copy-start.3
  194.7 3.1 %copy-start.2 = (f32[64,3328]{1,0:T(8,128)S(1)}, f32[64,3328]{1,0:T(8,128)}, u32[]{:S(2)}) copy-start(f32[64,3328]{1,0:T(8,128)} %fusion.36) | copy-start | bytes 2555908
  194.7 3.1 %copy-start.6 = (f32[1,64,64]{1,2,0:T(8,128)S(1)}, f32[1,64,64]{1,2,0:T(8,128)}, u32[]{:S(2)}) copy-start(f32[1,64,64]{1,2,0:T(8,128)} %custom-call.15) | copy-start | bytes 49156
  195.8 3.7 %copy-start.5 = (f32[512,64]{0,1:T(8,128)}, f32[512,64]{0,1:T(8,128)S(1)}, u32[]{:S(2)}) copy-start(f32[512,64]{0,1:T(8,128)S(1)} %convolution_bitcast_fusion) | copy-start | bytes 393220

commit v2 on v1

v2 whole, which is shorter than its diff:
```python
import functools
import math

import jax
import jax.numpy as jnp
from jax import lax
from jax.experimental import pallas as pl
from jax.experimental.pallas import tpu as pltpu
from jax.sharding import Mesh, PartitionSpec as P

BLOCK = 128
HIGHEST = lax.Precision.HIGHEST
F32 = jnp.float32
BF16 = jnp.bfloat16
NT = (((1,), (1,)), ((), ()))
NN = (((1,), (0,)), ((), ()))


def dot(a, b, dims=NN, precision=None):
    return lax.dot_general(a, b, dims, precision=precision, preferred_element_type=F32)


def split3(x):
    high = x.astype(BF16)
    rest = x - high.astype(F32)
    middle = rest.astype(BF16)
    low = (rest - middle.astype(F32)).astype(BF16)
    return high, middle, low


def gram_beside_identity(rows):
    rank = rows.shape[0]
    both = jnp.concatenate([jnp.zeros_like(rows), rows], axis=0)
    gram = dot(rows, both, NT, HIGHEST)
    lane = lax.broadcasted_iota(jnp.int32, (rank, 2 * rank), 1)
    row = lax.broadcasted_iota(jnp.int32, (rank, 2 * rank), 0)
    return gram + (lane == row).astype(F32)


def eliminate(table, out):
    rank, width = table.shape
    rest = table
    for p in range(0, rank, 8):
        high = rank - p
        columns = [
            jnp.broadcast_to(rest[:, rank + p + j : rank + p + j + 1], (high, width))
            for j in range(8)
        ]
        for j in range(8):
            column = columns[j]
            pivot = column[j : j + 1, :]
            root = lax.rsqrt(pivot)
            inverse = 1.0 / pivot
            row = rest[j : j + 1, :]
            out[p + j : p + j + 1, :] = row * root
            scaled = row * inverse
            for i in range(j + 1, 8):
                columns[i] = columns[i] - column * (columns[i][j : j + 1, :] * inverse)
            rest = rest - column * scaled
        rest = rest[8:, :]


def sweep(rows, table):
    rank = rows.shape[0]
    eliminate(gram_beside_identity(rows), table)
    return dot(table[:, :rank], rows, NN, HIGHEST)


def factor_kernel(scale, packed, sketch, weights, basis, parts, table):
    rank, width = sketch.shape
    n = width // BLOCK
    at = 0
    for i in range(n):
        for j in range(i, n):
            block = packed[at : at + BLOCK, :]
            at += BLOCK
            for k, part in enumerate(split3(block)):
                parts[k, i * BLOCK : (i + 1) * BLOCK, j * BLOCK : (j + 1) * BLOCK] = part
            if j > i:
                for k, part in enumerate(split3(block.T)):
                    parts[k, j * BLOCK : (j + 1) * BLOCK, i * BLOCK : (i + 1) * BLOCK] = part

    def times_gram(rows):
        return (dot(rows, parts[2]) + dot(rows, parts[1])) + dot(rows, parts[0])

    wide = times_gram(sketch[...])
    estimate = sweep(sweep(wide, table), table).astype(BF16)
    near = estimate.astype(F32)
    image = times_gram(estimate)
    both = jnp.concatenate([jnp.zeros_like(near), near], axis=0)
    gram = dot(image, both, NT, HIGHEST)
    lane = lax.broadcasted_iota(jnp.int32, (rank, 2 * rank), 1)
    row = lax.broadcasted_iota(jnp.int32, (rank, 2 * rank), 0)
    eliminate(gram + (lane == row).astype(F32), table)
    inverse = table[:, :rank]
    for k, part in enumerate(split3(dot(inverse, near, NN, HIGHEST) * scale)):
        weights[k * rank : (k + 1) * rank, :] = part
    projected = dot(inverse, image, NN, HIGHEST)
    base = sweep(sweep(projected, table), table)
    basis[...] = base
    weights[3 * rank : 4 * rank, :] = base.astype(BF16)


def factor(packed, sketch_rows, scale):
    rank, width = sketch_rows.shape
    return pl.pallas_call(
        functools.partial(factor_kernel, scale),
        out_shape=(
            jax.ShapeDtypeStruct((4 * rank, width), BF16),
            jax.ShapeDtypeStruct((rank, width), F32),
        ),
        in_specs=[pl.BlockSpec(memory_space=pltpu.VMEM)] * 2,
        out_specs=(pl.BlockSpec(memory_space=pltpu.VMEM),) * 2,
        scratch_shapes=[
            pltpu.VMEM((3, width, width), BF16),
            pltpu.VMEM((rank, 2 * rank), F32),
        ],
        compiler_params=pltpu.CompilerParams(vmem_limit_bytes=32 * 1024 * 1024),
        name="factor",
    )(packed, sketch_rows)


def apply_kernel(features, weights, left, codes):
    rank = left.shape[0]
    out = dot(weights[...], features[...], NT)
    left[...] = (out[2 * rank : 3 * rank] + out[rank : 2 * rank]) + out[:rank]
    codes[...] = out[3 * rank :].astype(BF16)


def apply(features, weights, step):
    rows, width = features.shape
    rank = weights.shape[0] // 4
    return pl.pallas_call(
        apply_kernel,
        grid=(rows // step,),
        out_shape=(
            jax.ShapeDtypeStruct((rank, rows), F32),
            jax.ShapeDtypeStruct((rank, rows), BF16),
        ),
        in_specs=[
            pl.BlockSpec((step, width), lambda i: (i, 0)),
            pl.BlockSpec((4 * rank, width), lambda i: (0, 0)),
        ],
        out_specs=(
            pl.BlockSpec((rank, step), lambda i: (0, i)),
            pl.BlockSpec((rank, step), lambda i: (0, i)),
        ),
        compiler_params=pltpu.CompilerParams(vmem_limit_bytes=32 * 1024 * 1024),
        name="apply",
    )(features, weights)


def gram_kernel(features, packed):
    width = features.shape[1]
    n = width // BLOCK

    @pl.when(pl.program_id(0) == 0)
    def _():
        packed[...] = jnp.zeros_like(packed)

    f = features[...]
    dims = (((0,), (0,)), ((), ()))
    half = width // 2
    top = dot(f[:, :half], f, dims)
    bottom = dot(f[:, half:], f[:, half:], dims)
    at = 0
    for i in range(n):
        for j in range(i, n):
            if i < n // 2:
                src = top[i * BLOCK : (i + 1) * BLOCK, j * BLOCK : (j + 1) * BLOCK]
            else:
                a, b = i - n // 2, j - n // 2
                src = bottom[a * BLOCK : (a + 1) * BLOCK, b * BLOCK : (b + 1) * BLOCK]
            packed[at : at + BLOCK, :] += src
            at += BLOCK


def local_gram(features, step):
    rows, width = features.shape
    n = width // BLOCK
    return pl.pallas_call(
        gram_kernel,
        grid=(rows // step,),
        out_shape=jax.ShapeDtypeStruct((n * (n + 1) // 2 * BLOCK, BLOCK), F32),
        in_specs=[pl.BlockSpec((step, width), lambda i: (i, 0))],
        out_specs=pl.BlockSpec((n * (n + 1) // 2 * BLOCK, BLOCK), lambda i: (0, 0)),
        compiler_params=pltpu.CompilerParams(vmem_limit_bytes=32 * 1024 * 1024),
        name="gram",
    )(features)


def exchange(parts, axes):
    return lax.all_to_all(parts, axes, split_axis=0, concat_axis=0, tiled=True)


def sum_everywhere(packed):
    plane = lax.axis_size(("gx", "c"))
    rows, width = packed.shape
    share = jnp.sum(exchange(packed.reshape(plane, rows // plane, width), ("gx", "c")), axis=0)
    line = lax.axis_size("z")
    share = jnp.sum(exchange(jnp.broadcast_to(share, (line, *share.shape)), "z"), axis=0)
    whole = exchange(jnp.broadcast_to(share, (plane, *share.shape)), ("gx", "c"))
    return whole.reshape(rows, width)


def on_device(features, sketch):
    scale = math.sqrt(features.shape[0] * lax.axis_size(("gx", "z", "c")))
    step = features.shape[0] // 2
    packed = sum_everywhere(local_gram(features, step))
    weights, basis = factor(packed, sketch.T, scale)
    left, codes = apply(features, weights, step)
    return (basis.T, codes.T, left.T)


def solution(mesh):
    rows, columns = mesh.devices.shape
    mesh = Mesh(mesh.devices.reshape(rows, columns // 2, 2), ("gx", "z", "c"))
    split = P(("gx", "z", "c"), None)
    return jax.shard_map(
        on_device,
        mesh=mesh,
        in_specs=(split, P()),
        out_specs=(P(), split, split),
        check_vma=False,
    )
```

time: 202 us -> 96.7 us (0.48); the launches traced: 200 us -> 96.4 us
  other arithmetic: 85.5 us -> 2.14 us
  matrix products: 19.9 us -> 0 us
  Pallas kernels: 0 us -> 17 us
  local copies, waits for them, and re-layouts: 18.9 us -> 2.04 us
    another operation x25 -> x0, other arithmetic: 76.3 us -> none  [the longest x10 37.3 us: solve_right(): lax.linalg.triangular_solve(factor, matrix, left_side=False, lower=True,...]
    pallas_call x0 -> x3, Pallas kernels: none -> 17 us  [the longest x1 12.9 us: factor(): pl.pallas_call(functools.partial(factor_kernel, scale), out_shape=(jax.Sh...]
    dot_general x10 -> x0, matrix products: 12.4 us -> none  [the longest x4 2.27 us: sweep(): gram = jnp.dot(matrix.T, matrix, precision=HIGHEST)]
    another operation x6 -> x0, matrix products: 7.55 us -> none  [solve_right(): lax.linalg.triangular_solve(factor, matrix, left_side=False, lower=True,...]
    unnamed x25 -> x6, local copies, waits for them, and re-layouts: 6.92 us -> 1.97 us
    transpose x3 -> x0, local copies, waits for them, and re-layouts: 4.67 us -> none  [unpack(): row = [blocks[i, j] if j >= i else blocks[j, i].T for j in range(n)]]
    dot_general x5 -> x0, local copies, waits for them, and re-layouts: 4.51 us -> none  [the longest x4 3.06 us: sweep(): gram = jnp.dot(matrix.T, matrix, precision=HIGHEST)]
    div x5 -> x0, other arithmetic: 4.2 us -> none  [the longest x4 2.81 us: sweep(): return solve_right(jnp.linalg.cholesky(gram), matrix)]
where the time goes in v2:
time: 96.7 us; the launch traced here: 96.4 us
  blocking collectives  74.6 us (77%)
  Pallas kernels  17 us (18%)
  other arithmetic  2.14 us (2%)
  local copies, waits for them, and re-layouts  2.04 us (2%)
    all_to_all x3, blocking collectives, exchange(): return lax.all_to_all(parts, axes, split_axis=0, concat_axis=0, tiled=True)  74.6 us
    pallas_call x1, Pallas kernels, factor(): pl.pallas_call(functools.partial(factor_kernel, scale), out_shape=(jax.Sh...  12.9 us
    pallas_call x1, Pallas kernels, apply(): pl.pallas_call(apply_kernel, grid=(rows // step,), out_shape=(jax.ShapeDt...  2.17 us
    unnamed x6, local copies, waits for them, and re-layouts  1.97 us

profile of v2, /device:TPU:1, one launch (start us, length us, event | category | flops | bytes accessed | tf_op | source)
XLA Modules:
  0.0 96.4 jit_solution(4071151084114539227)
XLA Ops:
  0.6 0.0 copy-start
  0.6 2.0 %copy-done = bf16[3328,512]{1,0:T(8,128)(2,1)S(1)} copy-done((bf16[3328,512]{1,0:T(8,128)(2,1)S(1)}, bf16[3328,512]{1,0:T(8,128)(2,1)}, u32[]{:S(2)}) %copy-start) | copy-done | bytes 3407896
  2.6 1.9 %gram.1 = f32[1280,128]{1,0:T(8,128)S(1)} custom-call(bf16[3328,512]{1,0:T(8,128)(2,1)S(1)} %copy-done), custom_call_target="tpu_custom_call" | custom-call | tf_op jit(solution)/shard_map/gram/pallas_call | solution.py:181
  4.5 0.0 copy-start.2
  4.5 0.0 copy-start.1
  4.5 23.5 %all_to_all.15 = f32[32,40,128]{2,1,0:T(8,128)} all-to-all(f32[32,40,128]{2,1,0:T(8,128)S(1)} %bitcast.6), channel_id=1, replica_groups=mesh['gx'=16,'z'=16,'c'=2] {'gx','c'}, dimensions={0} | all-to-all | bytes 1310720 | tf_op jit(solution)/shard_map/all_to_all | solution.py:193
  28.0 1.1 %reduce_sum.18 = f32[40,128]{1,0:T(8,128)S(1)} reduce(f32[32,40,128]{2,1,0:T(8,128)} %all_to_all.15, f32[]{:T(128)} %constant.0.clone.1), dimensions={0}, to_apply=%region_0.0 | reduce | flops 158720 | bytes 675844 | tf_op jit(solution)/shard_map/reduce_sum | solution.py:199
  29.2 31.2 %all_to_all.16 = f32[16,40,128]{2,1,0:T(8,128)} all-to-all(f32[16,40,128]{2,1,0:T(8,128)S(1)} %broadcast_in_dim.6), channel_id=1, replica_groups=mesh['gx'=16,'z'=16,'c'=2] {'z'}, dimensions={0} | all-to-all | bytes 655360 | tf_op jit(solution)/shard_map/all_to_all | solution.py:193
  60.4 1.0 %reduce_sum.19 = f32[40,128]{1,0:T(8,128)S(1)} reduce(f32[16,40,128]{2,1,0:T(8,128)} %all_to_all.16, f32[]{:T(128)} %constant.0.clone.1), dimensions={0}, to_apply=%region_1.0 | reduce | flops 76800 | bytes 348164 | tf_op jit(solution)/shard_map/reduce_sum | solution.py:201
  61.4 19.9 %all_to_all.17 = f32[32,40,128]{2,1,0:T(8,128)S(1)} all-to-all(f32[32,40,128]{2,1,0:T(8,128)S(1)} %broadcast_in_dim.7), channel_id=1, replica_groups=mesh['gx'=16,'z'=16,'c'=2] {'gx','c'}, dimensions={0} | all-to-all | bytes 1310720 | tf_op jit(solution)/shard_map/all_to_all | solution.py:193
  81.3 0.0 copy-done.2
  81.3 12.9 %factor.1 = (bf16[256,512]{1,0:T(8,128)(2,1)S(1)}, f32[64,512]{1,0:T(8,128)}) custom-call(f32[1280,128]{1,0:T(8,128)S(1)} %bitcast.7, bf16[64,512]{1,0:T(8,128)(2,1)S(1)} %bitcast.8), custom_call_target="tpu_custom_call" | custom-call | tf_op jit(solution)/shard_map/factor/pallas_call | solution.py:106
  94.3 0.0 copy-done.1
  94.3 2.2 %apply.1 = (f32[64,3328]{1,0:T(8,128)}, bf16[64,3328]{1,0:T(8,128)(2,1)}) custom-call(bf16[3328,512]{1,0:T(8,128)(2,1)S(1)} %copy-done.1, bf16[256,512]{1,0:T(8,128)(2,1)S(1)} %get-tuple-element.8.weights), custom_call_target="tpu_custom_call" | custom-call | tf_op jit(solution)/shard_map/apply/pallas_call | solution.py:133
  (2 shorter events, 0.1 us)
Async XLA Ops:
  0.6 2.0 %copy-start = (bf16[3328,512]{1,0:T(8,128)(2,1)S(1)}, bf16[3328,512]{1,0:T(8,128)(2,1)}, u32[]{:S(2)}) copy-start(bf16[3328,512]{1,0:T(8,128)(2,1)} %features.3) | copy-start | bytes 10223620
  4.5 76.8 %copy-start.2 = (bf16[512,64]{0,1:T(8,128)(2,1)S(1)}, bf16[512,64]{0,1:T(8,128)(2,1)}, u32[]{:S(2)}) copy-start(bf16[512,64]{0,1:T(8,128)(2,1)} %param.3) | copy-start | bytes 196612
  4.5 89.7 %copy-start.1 = (bf16[3328,512]{1,0:T(8,128)(2,1)S(1)}, bf16[3328,512]{1,0:T(8,128)(2,1)}, u32[]{:S(2)}) copy-start(bf16[3328,512]{1,0:T(8,128)(2,1)} %features.3) | copy-start | bytes 10223620

commit v3 on v0

v3 whole, which is shorter than its diff:
```python
import functools
import math

import jax
import jax.numpy as jnp
from jax import lax
from jax.experimental import pallas as pl
from jax.experimental.pallas import tpu as pltpu
from jax.sharding import Mesh, PartitionSpec as P

BLOCK = 128
ROOM = 24 * 1024 * 1024
HIGHEST = lax.Precision.HIGHEST
F32 = jnp.float32
BF16 = jnp.bfloat16
NT = (((1,), (1,)), ((), ()))
NN = (((1,), (0,)), ((), ()))
TN = (((0,), (0,)), ((), ()))


def dot(a, b, dims=NN, precision=None):
    return lax.dot_general(a, b, dims, precision=precision, preferred_element_type=F32)


def split3(x):
    high = x.astype(BF16)
    rest = x - high.astype(F32)
    middle = rest.astype(BF16)
    low = (rest - middle.astype(F32)).astype(BF16)
    return high, middle, low


def upper_blocks(n):
    return [(i, j) for i in range(n) for j in range(i, n)]


def cuts(rows, weights):
    units = rows // BLOCK
    total = sum(weights)
    edges = [0]
    for k in range(len(weights)):
        edges.append(round(units * sum(weights[: k + 1]) / total) * BLOCK)
    return list(zip(edges[:-1], edges[1:]))


def gram_kernel(plan, core_of, features, keep, send, held, arrived):
    width = features.shape[1]
    n = width // BLOCK
    half = width // 2
    copies = []
    for k, (start, stop) in enumerate(plan):
        rows = pl.ds(start, stop - start)
        copies.append(pltpu.make_async_copy(features.at[rows], held.at[rows], arrived.at[k]))
    for copy in copies[:2]:
        copy.start()
    core = core_of()
    top = bottom = None
    for k, (start, stop) in enumerate(plan):
        copies[k].wait()
        if k + 2 < len(copies):
            copies[k + 2].start()
        f = held[start:stop, :]
        a = dot(f[:, :half], f, TN)
        b = dot(f[:, half:], f[:, half:], TN)
        top = a if top is None else top + a
        bottom = b if bottom is None else bottom + b
    pieces = []
    for i, j in upper_blocks(n):
        if i < n // 2:
            src, a, b = top, i, j
        else:
            src, a, b = bottom, i - n // 2, j - n // 2
        pieces.append(src[a * BLOCK : (a + 1) * BLOCK, b * BLOCK : (b + 1) * BLOCK])
    count = len(pieces) // 2
    for k in range(count):
        rows = slice(k * BLOCK, (k + 1) * BLOCK)
        keep[rows, :] = jnp.where(core == 0, pieces[k], pieces[count + k])
        send[rows, :] = jnp.where(core == 0, pieces[count + k], pieces[k])


def local_gram(features, core_of, weights=(1, 1, 1)):
    rows, width = features.shape
    n = width // BLOCK
    half = jax.ShapeDtypeStruct((n * (n + 1) // 4 * BLOCK, BLOCK), F32)
    plan = cuts(rows, weights)
    return pl.pallas_call(
        functools.partial(gram_kernel, plan, core_of),
        out_shape=(half, half),
        in_specs=[pl.BlockSpec(memory_space=pl.ANY)],
        out_specs=(pl.BlockSpec(memory_space=pltpu.VMEM),) * 2,
        scratch_shapes=[
            pltpu.VMEM((rows, width), BF16),
            pltpu.SemaphoreType.DMA((len(plan),)),
        ],
        compiler_params=pltpu.CompilerParams(vmem_limit_bytes=ROOM),
        cost_estimate=pl.CostEstimate(
            flops=2 * rows * width * width, bytes_accessed=2 * rows * width, transcendentals=0
        ),
        name="gram",
    )(pltpu.with_memory_space_constraint(features, pltpu.HBM))


def beside_identity(gram, rank):
    lane = lax.broadcasted_iota(jnp.int32, (rank, 2 * rank), 1)
    row = lax.broadcasted_iota(jnp.int32, (rank, 2 * rank), 0)
    return gram + (lane == row).astype(F32)


def gram_of(a, b):
    both = jnp.concatenate([jnp.zeros_like(b), b], axis=0)
    return beside_identity(dot(a, both, NT, HIGHEST), a.shape[0])


def eliminate(tables, outs):
    rank, width = tables[0].shape
    rests = list(tables)
    for p in range(0, rank, 8):
        high = rank - p
        panels = [
            [
                jnp.broadcast_to(rest[:, rank + p + j : rank + p + j + 1], (high, width))
                for j in range(8)
            ]
            for rest in rests
        ]
        for j in range(8):
            for t, out in enumerate(outs):
                columns, rest = panels[t], rests[t]
                column = columns[j]
                pivot = column[j : j + 1, :]
                inverse = 1.0 / pivot
                row = rest[j : j + 1, :]
                out[p + j : p + j + 1, :] = row * lax.rsqrt(pivot)
                for i in range(j + 1, 8):
                    columns[i] = columns[i] - column * (columns[i][j : j + 1, :] * inverse)
                rests[t] = rest - column * (row * inverse)
        rests = [rest[8:, :] for rest in rests]


def nearly_identity(rows):
    rank = rows.shape[0]
    lane = lax.broadcasted_iota(jnp.int32, (rank, rank), 1)
    row = lax.broadcasted_iota(jnp.int32, (rank, rank), 0)
    eye = (lane == row).astype(F32)
    half = jnp.where(lane < row, 1.0, 0.0) + 0.5 * eye
    off = dot(rows, rows, NT, HIGHEST) - eye
    first = off * half
    square = dot(first, first, NN, HIGHEST)
    outer = dot(first, first, NT, HIGHEST) * half
    return jnp.sum(off * off), eye + ((square + outer) - first)


def finish_kernel(
    scale, plan, core_of, mine, other, sketch, features, basis, left, codes,
    parts, table, image_table, hold, weights, held, left_held, codes_held, arrived, gone,
):
    rank, width = sketch.shape
    n = width // BLOCK
    fetches = []
    for k, (start, stop) in enumerate(plan):
        rows = pl.ds(start, stop - start)
        copy = pltpu.make_async_copy(features.at[rows], held.at[rows], arrived.at[k])
        copy.start()
        fetches.append(copy)
    core = core_of()
    blocks = upper_blocks(n)
    count = len(blocks) // 2
    for k, (i, j) in enumerate(blocks):
        rows = slice(k % count * BLOCK, (k % count + 1) * BLOCK)
        block = jnp.where(core == k // count, mine[rows, :], other[rows, :])
        for q, part in enumerate(split3(block)):
            parts[q, i * BLOCK : (i + 1) * BLOCK, j * BLOCK : (j + 1) * BLOCK] = part
        if j > i:
            for q, part in enumerate(split3(block.T)):
                parts[q, j * BLOCK : (j + 1) * BLOCK, i * BLOCK : (i + 1) * BLOCK] = part

    def times_gram(rows):
        return (dot(rows, parts[2]) + dot(rows, parts[1])) + dot(rows, parts[0])

    def sweep(rows):
        eliminate([gram_of(rows, rows)], [table])
        return dot(table[:, :rank], rows, NN, HIGHEST)

    wide = sweep(times_gram(sketch[...]))
    distance, inverse = nearly_identity(wide)
    hold[...] = dot(inverse, wide, NN, HIGHEST)

    @pl.when(jnp.logical_not(distance <= 1e-5))
    def _():
        hold[...] = sweep(wide)

    estimate = hold[...].astype(BF16)
    near = estimate.astype(F32)
    image = times_gram(estimate)
    eliminate([gram_of(image, near), gram_of(image, image)], [table, image_table])
    factor = table[:, :rank]
    for k, part in enumerate(split3(dot(factor, near, NN, HIGHEST) * scale)):
        weights[k * rank : (k + 1) * rank, :] = part
    swept = dot(image_table[:, :rank], image, NN, HIGHEST)
    distance, inverse = nearly_identity(swept)
    hold[...] = dot(inverse, swept, NN, HIGHEST)

    @pl.when(jnp.logical_not(distance <= 1e-5))
    def _():
        hold[...] = sweep(sweep(dot(factor, image, NN, HIGHEST)))

    basis[...] = hold[...]
    weights[3 * rank : 4 * rank, :] = hold[...].astype(BF16)

    sends = []
    for k, (start, stop) in enumerate(plan):
        fetches[k].wait()
        columns = slice(start, stop)
        out = dot(weights[...], held[start:stop, :], NT)
        left_held[:, columns] = (out[2 * rank : 3 * rank] + out[rank : 2 * rank]) + out[:rank]
        codes_held[:, columns] = out[3 * rank :].astype(BF16)
        span = pl.ds(start, stop - start)
        for q, (source, target) in enumerate(((left_held, left), (codes_held, codes))):
            copy = pltpu.make_async_copy(source.at[:, span], target.at[:, span], gone.at[q, k])
            copy.start()
            sends.append(copy)
    for copy in sends:
        copy.wait()


def finish(mine, other, sketch_rows, features, scale, core_of, weights=(1,)):
    rank, width = sketch_rows.shape
    rows = features.shape[0]
    plan = cuts(rows, weights)
    vmem = pl.BlockSpec(memory_space=pltpu.VMEM)
    hbm = pl.BlockSpec(memory_space=pl.ANY)
    return pl.pallas_call(
        functools.partial(finish_kernel, scale, plan, core_of),
        out_shape=(
            jax.ShapeDtypeStruct((rank, width), F32),
            jax.ShapeDtypeStruct((rank, rows), F32),
            jax.ShapeDtypeStruct((rank, rows), BF16),
        ),
        in_specs=[vmem, vmem, vmem, hbm],
        out_specs=(vmem, hbm, hbm),
        scratch_shapes=[
            pltpu.VMEM((3, width, width), BF16),
            pltpu.VMEM((rank, 2 * rank), F32),
            pltpu.VMEM((rank, 2 * rank), F32),
            pltpu.VMEM((rank, width), F32),
            pltpu.VMEM((4 * rank, width), BF16),
            pltpu.VMEM((rows, width), BF16),
            pltpu.VMEM((rank, rows), F32),
            pltpu.VMEM((rank, rows), BF16),
            pltpu.SemaphoreType.DMA((len(plan),)),
            pltpu.SemaphoreType.DMA((2, len(plan))),
        ],
        compiler_params=pltpu.CompilerParams(vmem_limit_bytes=ROOM),
        name="finish",
    )(mine, other, sketch_rows, pltpu.with_memory_space_constraint(features, pltpu.HBM))


def exchange(parts, axes):
    return lax.all_to_all(parts, axes, split_axis=0, concat_axis=0, tiled=True)


def swap(x):
    return lax.ppermute(x, "c", [(0, 1), (1, 0)])


def sum_everywhere(keep, send):
    chips, line = lax.axis_size("gx"), lax.axis_size("z")
    half = keep + swap(send)
    rows, width = half.shape
    share = jnp.sum(exchange(half.reshape(chips, rows // chips, width), "gx"), axis=0)
    share = jnp.sum(exchange(jnp.broadcast_to(share, (line, *share.shape)), "z"), axis=0)
    mine = exchange(jnp.broadcast_to(share, (chips, *share.shape)), "gx").reshape(rows, width)
    return mine, swap(mine)


def core_index():
    return lax.axis_index("c")


def on_device(features, sketch):
    scale = math.sqrt(features.shape[0] * lax.axis_size(("gx", "z", "c")))
    mine, other = sum_everywhere(*local_gram(features, core_index))
    basis, left, codes = finish(mine, other, sketch.T, features, scale, core_index)
    return (basis.T, codes.T, left.T)


def solution(mesh):
    rows, columns = mesh.devices.shape
    mesh = Mesh(mesh.devices.reshape(rows, columns // 2, 2), ("gx", "z", "c"))
    split = P(("gx", "z", "c"), None)
    return jax.shard_map(
        on_device,
        mesh=mesh,
        in_specs=(split, P()),
        out_specs=(P(), split, split),
        check_vma=False,
    )
```

time: 1110 us -> 87 us (0.08)
  waiting for transfers between devices: 893 us -> 2.47 us
  other arithmetic: 74.2 us -> 0.1 us
  blocking collectives: 100 us -> 49.4 us
  matrix products: 21.7 us -> 0 us
  starting transfers between devices: 0.08 us -> 20.3 us
  Pallas kernels: 0 us -> 13.7 us
  between operations: 14.2 us -> 0.68 us
    psum x2 -> x0, waiting for transfers between devices: 893 us -> none  [the longest x1 454 us: on_device(): wide = lax.psum(left_product(features, first), ('gx', 'gy'))]
    psum x1 -> x0, blocking collectives: 100 us -> none  [on_device(): lax.psum(jnp.dot(second.T, second, precision=lax.Precision.HIGHEST), ('gx...]
    another operation x25 -> x0, other arithmetic: 71.4 us -> none  [the longest x10 34.5 us: solve_right(): lax.linalg.triangular_solve(factor, matrix, left_side=False, lower=True,...]
    all_to_all x0 -> x3, blocking collectives: none -> 49.4 us  [exchange(): return lax.all_to_all(parts, axes, split_axis=0, concat_axis=0, tiled=True)]
    ppermute x0 -> x2, starting transfers between devices: none -> 20.3 us  [swap(): return lax.ppermute(x, 'c', [(0, 1), (1, 0)])]
    dot_general x12 -> x0, matrix products: 14.2 us -> none  [the longest x4 4.22 us: orthonormal(): gram = jnp.dot(matrix.T, matrix, precision=lax.Precision.HIGHEST)]
    pallas_call x0 -> x2, Pallas kernels: none -> 13.7 us  [the longest x1 10.1 us: finish(): pl.pallas_call(functools.partial(finish_kernel, scale, plan, core_of), ou...]
where the time goes in v3:
time: 87 us; the launch traced here: 86.7 us
  blocking collectives  49.4 us (57%)
  starting transfers between devices  20.3 us (23%)
  Pallas kernels  13.7 us (16%)
  waiting for transfers between devices  2.47 us (3%)
    all_to_all x3, blocking collectives, exchange(): return lax.all_to_all(parts, axes, split_axis=0, concat_axis=0, tiled=True)  49.4 us
    ppermute x2, starting transfers between devices, swap(): return lax.ppermute(x, 'c', [(0, 1), (1, 0)])  20.3 us
    pallas_call x1, Pallas kernels, finish(): pl.pallas_call(functools.partial(finish_kernel, scale, plan, core_of), ou...  10.1 us
    pallas_call x1, Pallas kernels, local_gram(): pl.pallas_call(functools.partial(gram_kernel, plan, core_of), out_shape=(...  3.62 us
    ppermute x2, waiting for transfers between devices, swap(): return lax.ppermute(x, 'c', [(0, 1), (1, 0)])  2.47 us
  transfers between devices with their start and end apart: 2, of which 2 were waited for; matrix products, arithmetic and copies ran while one was open for 0% of the time, Pallas kernels for 0%

profile of v3, /device:TPU:1, one launch (start us, length us, event | category | flops | bytes accessed | tf_op | source)
XLA Modules:
  0.0 86.7 jit_solution(15143752641631835157)
XLA Ops:
  0.6 3.6 %gram.1 = (f32[640,128]{1,0:T(8,128)S(1)}, f32[640,128]{1,0:T(8,128)S(1)}) custom-call(bf16[3328,512]{1,0:T(8,128)(2,1)} %features.3), custom_call_target="tpu_custom_call" | custom-call | flops 1744830464 | bytes 3407872 | tf_op jit(solution)/shard_map/gram/pallas_call | solution.py:86
  4.3 0.0 copy-start
  4.3 8.9 %collective-permute-start = (f32[640,128]{1,0:T(8,128)S(1)}, f32[640,128]{1,0:T(8,128)S(1)}, u32[]{:S(2)}, u32[]{:S(2)}) collective-permute-start(f32[640,128]{1,0:T(8,128)S(1)} %get-tuple-element.9), channel_id=1, source_target_pairs={{0,1},{1,0},{2,3},{3,2},{4,5},{5,4},{6,7},{7,6},{8,9},{9,8},{10,11... | collective-permute-start | bytes 983048 | tf_op jit(solution)/shard_map/ppermute | solution.py:263
  13.2 1.2 %collective-permute-done = f32[640,128]{1,0:T(8,128)S(1)} collective-permute-done((f32[640,128]{1,0:T(8,128)S(1)}, f32[640,128]{1,0:T(8,128)S(1)}, u32[]{:S(2)}, u32[]{:S(2)}) %collective-permute-start) | collective-permute-done | bytes 327712 | tf_op jit(solution)/shard_map/ppermute | solution.py:263
  14.5 11.2 %all_to_all.15 = f32[16,40,128]{2,1,0:T(8,128)S(1)} all-to-all(f32[16,40,128]{2,1,0:T(8,128)S(1)} %bitcast.9), channel_id=1, replica_groups=mesh['gx'=16,'z'=16,'c'=2] {'gx'}, dimensions={0} | all-to-all | bytes 655360 | tf_op jit(solution)/shard_map/all_to_all | solution.py:259
  25.8 26.2 %all_to_all.16 = f32[16,40,128]{2,1,0:T(8,128)S(1)} all-to-all(f32[16,40,128]{2,1,0:T(8,128)S(1)} %broadcast_in_dim.6), channel_id=1, replica_groups=mesh['gx'=16,'z'=16,'c'=2] {'z'}, dimensions={0} | all-to-all | bytes 655360 | tf_op jit(solution)/shard_map/all_to_all | solution.py:259
  52.1 11.9 %all_to_all.17 = f32[16,40,128]{2,1,0:T(8,128)S(1)} all-to-all(f32[16,40,128]{2,1,0:T(8,128)S(1)} %broadcast_in_dim.7), channel_id=1, replica_groups=mesh['gx'=16,'z'=16,'c'=2] {'gx'}, dimensions={0} | all-to-all | bytes 655360 | tf_op jit(solution)/shard_map/all_to_all | solution.py:259
  64.0 11.4 %collective-permute-start.1 = (f32[640,128]{1,0:T(8,128)S(1)}, f32[640,128]{1,0:T(8,128)S(1)}, u32[]{:S(2)}, u32[]{:S(2)}) collective-permute-start(f32[640,128]{1,0:T(8,128)S(1)} %bitcast.6), channel_id=1, source_target_pairs={{0,1},{1,0},{2,3},{3,2},{4,5},{5,4},{6,7},{7,6},{8,9},{9,8},{10,11... | collective-permute-start | bytes 983048 | tf_op jit(solution)/shard_map/ppermute | solution.py:263
  75.4 1.2 %collective-permute-done.1.other = f32[640,128]{1,0:T(8,128)S(1)} collective-permute-done((f32[640,128]{1,0:T(8,128)S(1)}, f32[640,128]{1,0:T(8,128)S(1)}, u32[]{:S(2)}, u32[]{:S(2)}) %collective-permute-start.1) | collective-permute-done | bytes 327712 | tf_op jit(solution)/shard_map/ppermute | solution.py:263
  76.6 0.0 copy-done
  76.6 10.1 %finish.1 = (f32[64,512]{1,0:T(8,128)}, f32[64,3328]{1,0:T(8,128)}, bf16[64,3328]{1,0:T(8,128)(2,1)}) custom-call(f32[640,128]{1,0:T(8,128)S(1)} %bitcast.7, f32[640,128]{1,0:T(8,128)S(1)} %collective-permute-done.1.other, bf16[64,512]{1,0:T(8,128)(2,1)S(1)} %bitcast.8, bf16[3328,512]{1,0:T(8,128)(2,1)} %features.3), custom_call_target="tpu_custom_call" | custom-call | tf_op jit(solution)/shard_map/finish/pallas_call | solution.py:232
  (5 shorter events, 0.1 us)
Async XLA Ops:
  4.3 72.3 %copy-start = (bf16[512,64]{0,1:T(8,128)(2,1)S(1)}, bf16[512,64]{0,1:T(8,128)(2,1)}, u32[]{:S(2)}) copy-start(bf16[512,64]{0,1:T(8,128)(2,1)} %param.3) | copy-start | bytes 196612
  4.3 10.2 %collective-permute-start = (f32[640,128]{1,0:T(8,128)S(1)}, f32[640,128]{1,0:T(8,128)S(1)}, u32[]{:S(2)}, u32[]{:S(2)}) collective-permute-start(f32[640,128]{1,0:T(8,128)S(1)} %get-tuple-element.9), channel_id=1, source_target_pairs={{0,1},{1,0},{2,3},{3,2},{4,5},{5,4},{6,7},{7,6},{8,9},{9,8},{10,11... | collective-permute-start | bytes 983048 | tf_op jit(solution)/shard_map/ppermute | solution.py:263
  64.0 12.6 %collective-permute-start.1 = (f32[640,128]{1,0:T(8,128)S(1)}, f32[640,128]{1,0:T(8,128)S(1)}, u32[]{:S(2)}, u32[]{:S(2)}) collective-permute-start(f32[640,128]{1,0:T(8,128)S(1)} %bitcast.6), channel_id=1, source_target_pairs={{0,1},{1,0},{2,3},{3,2},{4,5},{5,4},{6,7},{7,6},{8,9},{9,8},{10,11... | collective-permute-start | bytes 983048 | tf_op jit(solution)/shard_map/ppermute | solution.py:263

commit v4 on v3

--- a/solution.py
+++ b/solution.py
@@ -30,8 +30,10 @@
     return high, middle, low
 
 
-def upper_blocks(n):
-    return [(i, j) for i in range(n) for j in range(i, n)]
+def layout(n):
+    pairs = [(i, j) for i in range(n) for j in range(i + 1, n)]
+    count = len(pairs) // 2
+    return (pairs[:count], (0, 1)), (pairs[count:], (2, 3))
 
 
 def cuts(rows, weights):
@@ -64,24 +66,35 @@
         b = dot(f[:, half:], f[:, half:], TN)
         top = a if top is None else top + a
         bottom = b if bottom is None else bottom + b
-    pieces = []
-    for i, j in upper_blocks(n):
-        if i < n // 2:
-            src, a, b = top, i, j
+    def block(i, j):
+        if i >= n // 2:
+            src, i, j = bottom, i - n // 2, j - n // 2
         else:
-            src, a, b = bottom, i - n // 2, j - n // 2
-        pieces.append(src[a * BLOCK : (a + 1) * BLOCK, b * BLOCK : (b + 1) * BLOCK])
-    count = len(pieces) // 2
-    for k in range(count):
-        rows = slice(k * BLOCK, (k + 1) * BLOCK)
-        keep[rows, :] = jnp.where(core == 0, pieces[k], pieces[count + k])
-        send[rows, :] = jnp.where(core == 0, pieces[count + k], pieces[k])
-
-
-def local_gram(features, core_of, weights=(1, 1, 1)):
+            src = top
+        return src[i * BLOCK : (i + 1) * BLOCK, j * BLOCK : (j + 1) * BLOCK]
+
+    halves = []
+    for pairs, (a, b) in layout(n):
+        low = lax.broadcasted_iota(jnp.int32, (BLOCK // 2, BLOCK), 1) < BLOCK // 2
+        first, second = block(a, a), block(b, b)
+        corner = pltpu.roll(first[BLOCK // 2 :], BLOCK // 2, 1)
+        corners = jnp.where(low, corner, second[BLOCK // 2 :])
+        halves.append(
+            [block(*pair) for pair in pairs]
+            + [first[: BLOCK // 2], second[: BLOCK // 2], corners]
+        )
+    at = 0
+    for zero, one in zip(*halves):
+        rows = slice(at, at + zero.shape[0])
+        keep[rows, :] = jnp.where(core == 0, zero, one)
+        send[rows, :] = jnp.where(core == 0, one, zero)
+        at += zero.shape[0]
+
+
+def local_gram(features, core_of, weights=(1, 1)):
     rows, width = features.shape
     n = width // BLOCK
-    half = jax.ShapeDtypeStruct((n * (n + 1) // 4 * BLOCK, BLOCK), F32)
+    half = jax.ShapeDtypeStruct((n * (2 * n + 1) * BLOCK // 8, BLOCK), F32)
     plan = cuts(rows, weights)
     return pl.pallas_call(
         functools.partial(gram_kernel, plan, core_of),
@@ -163,16 +176,29 @@
         copy.start()
         fetches.append(copy)
     core = core_of()
-    blocks = upper_blocks(n)
-    count = len(blocks) // 2
-    for k, (i, j) in enumerate(blocks):
-        rows = slice(k % count * BLOCK, (k % count + 1) * BLOCK)
-        block = jnp.where(core == k // count, mine[rows, :], other[rows, :])
+
+    def store(i, j, block):
         for q, part in enumerate(split3(block)):
             parts[q, i * BLOCK : (i + 1) * BLOCK, j * BLOCK : (j + 1) * BLOCK] = part
-        if j > i:
-            for q, part in enumerate(split3(block.T)):
-                parts[q, j * BLOCK : (j + 1) * BLOCK, i * BLOCK : (i + 1) * BLOCK] = part
+
+    for half, (pairs, diagonal) in enumerate(layout(n)):
+
+        def rows_at(start, size):
+            rows = slice(start, start + size)
+            return jnp.where(core == half, mine[rows, :], other[rows, :])
+
+        for k, (i, j) in enumerate(pairs):
+            block = rows_at(k * BLOCK, BLOCK)
+            store(i, j, block)
+            store(j, i, block.T)
+        at = len(pairs) * BLOCK
+        corners = rows_at(at + BLOCK, BLOCK // 2)
+        for k, i in enumerate(diagonal):
+            corner = corners if k else pltpu.roll(corners, BLOCK // 2, 1)
+            block = jnp.concatenate([rows_at(at + k * BLOCK // 2, BLOCK // 2), corner], axis=0)
+            lane = lax.broadcasted_iota(jnp.int32, (BLOCK, BLOCK), 1)
+            row = lax.broadcasted_iota(jnp.int32, (BLOCK, BLOCK), 0)
+            store(i, i, jnp.where((row >= BLOCK // 2) & (lane < BLOCK // 2), block.T, block))
 
     def times_gram(rows):
         return (dot(rows, parts[2]) + dot(rows, parts[1])) + dot(rows, parts[0])
@@ -223,7 +249,7 @@
         copy.wait()
 
 
-def finish(mine, other, sketch_rows, features, scale, core_of, weights=(1,)):
+def finish(mine, other, sketch_rows, features, scale, core_of, weights=(5, 1)):
     rank, width = sketch_rows.shape
     rows = features.shape[0]
     plan = cuts(rows, weights)
@@ -264,12 +290,13 @@
 
 
 def sum_everywhere(keep, send):
-    chips, line = lax.axis_size("gx"), lax.axis_size("z")
+    slab, line = ("gx", "near"), "far"
+    cells, length = lax.axis_size(slab), lax.axis_size(line)
     half = keep + swap(send)
     rows, width = half.shape
-    share = jnp.sum(exchange(half.reshape(chips, rows // chips, width), "gx"), axis=0)
-    share = jnp.sum(exchange(jnp.broadcast_to(share, (line, *share.shape)), "z"), axis=0)
-    mine = exchange(jnp.broadcast_to(share, (chips, *share.shape)), "gx").reshape(rows, width)
+    share = jnp.sum(exchange(half.reshape(cells, rows // cells, 1, width), slab), axis=0)
+    share = jnp.sum(exchange(jnp.broadcast_to(share, (length, *share.shape)), line), axis=0)
+    mine = exchange(jnp.broadcast_to(share, (cells, *share.shape)), slab).reshape(rows, width)
     return mine, swap(mine)
 
 
@@ -278,7 +305,7 @@
 
 
 def on_device(features, sketch):
-    scale = math.sqrt(features.shape[0] * lax.axis_size(("gx", "z", "c")))
+    scale = math.sqrt(features.shape[0] * lax.axis_size(("gx", "far", "near", "c")))
     mine, other = sum_everywhere(*local_gram(features, core_index))
     basis, left, codes = finish(mine, other, sketch.T, features, scale, core_index)
     return (basis.T, codes.T, left.T)
@@ -286,8 +313,8 @@
 
 def solution(mesh):
     rows, columns = mesh.devices.shape
-    mesh = Mesh(mesh.devices.reshape(rows, columns // 2, 2), ("gx", "z", "c"))
-    split = P(("gx", "z", "c"), None)
+    mesh = Mesh(mesh.devices.reshape(rows, columns // 4, 2, 2), ("gx", "far", "near", "c"))
+    split = P(("gx", "far", "near", "c"), None)
     return jax.shard_map(
         on_device,
         mesh=mesh,

time: 87 us -> 82.5 us (0.948)
  starting transfers between devices: 20.3 us -> 15.4 us
    ppermute x2, starting transfers between devices: 20.3 us -> 15.4 us  [swap(): return lax.ppermute(x, 'c', [(0, 1), (1, 0)])]
where the time goes in v4:
time: 82.5 us; the launch traced here: 82.2 us
  blocking collectives  49.4 us (60%)
  starting transfers between devices  15.4 us (19%)
  Pallas kernels  13.7 us (17%)
  waiting for transfers between devices  2.37 us (3%)
  between operations  0.85 us (1%)
    all_to_all x3, blocking collectives, exchange(): return lax.all_to_all(parts, axes, split_axis=0, concat_axis=0, tiled=True)  49.4 us
    ppermute x2, starting transfers between devices, swap(): return lax.ppermute(x, 'c', [(0, 1), (1, 0)])  15.4 us
    pallas_call x1, Pallas kernels, finish(): pl.pallas_call(functools.partial(finish_kernel, scale, plan, core_of), ou...  10 us
    pallas_call x1, Pallas kernels, local_gram(): pl.pallas_call(functools.partial(gram_kernel, plan, core_of), out_shape=(...  3.67 us
    ppermute x2, waiting for transfers between devices, swap(): return lax.ppermute(x, 'c', [(0, 1), (1, 0)])  2.37 us
  transfers between devices with their start and end apart: 2, of which 2 were waited for; matrix products, arithmetic and copies ran while one was open for 0% of the time, Pallas kernels for 0%

profile of v4, /device:TPU:1, one launch (start us, length us, event | category | flops | bytes accessed | tf_op | source)
XLA Modules:
  0.0 82.2 jit_solution(2929333733500129951)
XLA Ops:
  0.6 0.0 copy-start
  0.6 3.7 %gram.1 = (f32[576,128]{1,0:T(8,128)S(1)}, f32[576,128]{1,0:T(8,128)S(1)}) custom-call(bf16[3328,512]{1,0:T(8,128)(2,1)} %features.3), custom_call_target="tpu_custom_call" | custom-call | flops 1744830464 | bytes 3407872 | tf_op jit(solution)/shard_map/gram/pallas_call | solution.py:99
  4.3 8.8 %collective-permute-start = (f32[576,128]{1,0:T(8,128)S(1)}, f32[576,128]{1,0:T(8,128)S(1)}, u32[]{:S(2)}, u32[]{:S(2)}) collective-permute-start(f32[576,128]{1,0:T(8,128)S(1)} %get-tuple-element.9), channel_id=1, source_target_pairs={{0,1},{1,0},{2,3},{3,2},{4,5},{5,4},{6,7},{7,6},{8,9},{9,8},{10,11... | collective-permute-start | bytes 884744 | tf_op jit(solution)/shard_map/ppermute | solution.py:289
  13.1 1.2 %collective-permute-done = f32[576,128]{1,0:T(8,128)S(1)} collective-permute-done((f32[576,128]{1,0:T(8,128)S(1)}, f32[576,128]{1,0:T(8,128)S(1)}, u32[]{:S(2)}, u32[]{:S(2)}) %collective-permute-start) | collective-permute-done | bytes 294944 | tf_op jit(solution)/shard_map/ppermute | solution.py:289
  14.3 12.2 %all_to_all.15 = f32[32,18,1,128]{3,2,1,0:T(1,128)S(1)} all-to-all(f32[32,18,1,128]{3,2,1,0:T(1,128)S(1)} %bitcast.9), channel_id=1, replica_groups=mesh['gx'=16,'far'=8,'near'=2,'c'=2] {'gx','near'}, dimensions={0} | all-to-all | bytes 589824 | tf_op jit(solution)/shard_map/all_to_all | solution.py:285
  26.6 0.2 reduce_sum.18
  26.8 25.4 %all_to_all.16 = f32[8,18,1,128]{3,2,1,0:T(1,128)S(1)} all-to-all(f32[8,18,1,128]{3,2,1,0:T(1,128)S(1)} %broadcast_in_dim.6), channel_id=1, replica_groups=mesh['gx'=16,'far'=8,'near'=2,'c'=2] {'far'}, dimensions={0} | all-to-all | bytes 147456 | tf_op jit(solution)/shard_map/all_to_all | solution.py:285
  52.2 0.1 reduce_sum.19
  52.3 0.2 broadcast_in_dim.7
  52.5 11.7 %all_to_all.17 = f32[32,18,1,128]{3,2,1,0:T(1,128)S(1)} all-to-all(f32[32,18,1,128]{3,2,1,0:T(1,128)S(1)} %broadcast_in_dim.7), channel_id=1, replica_groups=mesh['gx'=16,'far'=8,'near'=2,'c'=2] {'gx','near'}, dimensions={0} | all-to-all | bytes 589824 | tf_op jit(solution)/shard_map/all_to_all | solution.py:285
  64.2 6.6 %collective-permute-start.1 = (f32[576,128]{1,0:T(8,128)S(1)}, f32[576,128]{1,0:T(8,128)S(1)}, u32[]{:S(2)}, u32[]{:S(2)}) collective-permute-start(f32[576,128]{1,0:T(8,128)S(1)} %bitcast.6), channel_id=1, source_target_pairs={{0,1},{1,0},{2,3},{3,2},{4,5},{5,4},{6,7},{7,6},{8,9},{9,8},{10,11... | collective-permute-start | bytes 884744 | tf_op jit(solution)/shard_map/ppermute | solution.py:289
  70.8 1.2 %collective-permute-done.1.other = f32[576,128]{1,0:T(8,128)S(1)} collective-permute-done((f32[576,128]{1,0:T(8,128)S(1)}, f32[576,128]{1,0:T(8,128)S(1)}, u32[]{:S(2)}, u32[]{:S(2)}) %collective-permute-start.1) | collective-permute-done | bytes 294944 | tf_op jit(solution)/shard_map/ppermute | solution.py:289
  72.0 0.0 copy-done
  72.0 10.0 %finish.1 = (f32[64,512]{1,0:T(8,128)}, f32[64,3328]{1,0:T(8,128)}, bf16[64,3328]{1,0:T(8,128)(2,1)}) custom-call(f32[576,128]{1,0:T(8,128)S(1)} %bitcast.7, f32[576,128]{1,0:T(8,128)S(1)} %collective-permute-done.1.other, bf16[64,512]{1,0:T(8,128)(2,1)S(1)} %bitcast.8, bf16[3328,512]{1,0:T(8,128)(2,1)} %features.3), custom_call_target="tpu_custom_call" | custom-call | tf_op jit(solution)/shard_map/finish/pallas_call | solution.py:258
  (2 shorter events, 0.1 us)
Async XLA Ops:
  0.6 71.4 %copy-start = (bf16[512,64]{0,1:T(8,128)(2,1)S(1)}, bf16[512,64]{0,1:T(8,128)(2,1)}, u32[]{:S(2)}) copy-start(bf16[512,64]{0,1:T(8,128)(2,1)} %param.3) | copy-start | bytes 196612
  4.3 10.0 %collective-permute-start = (f32[576,128]{1,0:T(8,128)S(1)}, f32[576,128]{1,0:T(8,128)S(1)}, u32[]{:S(2)}, u32[]{:S(2)}) collective-permute-start(f32[576,128]{1,0:T(8,128)S(1)} %get-tuple-element.9), channel_id=1, source_target_pairs={{0,1},{1,0},{2,3},{3,2},{4,5},{5,4},{6,7},{7,6},{8,9},{9,8},{10,11... | collective-permute-start | bytes 884744 | tf_op jit(solution)/shard_map/ppermute | solution.py:289
  64.2 7.8 %collective-permute-start.1 = (f32[576,128]{1,0:T(8,128)S(1)}, f32[576,128]{1,0:T(8,128)S(1)}, u32[]{:S(2)}, u32[]{:S(2)}) collective-permute-start(f32[576,128]{1,0:T(8,128)S(1)} %bitcast.6), channel_id=1, source_target_pairs={{0,1},{1,0},{2,3},{3,2},{4,5},{5,4},{6,7},{7,6},{8,9},{9,8},{10,11... | collective-permute-start | bytes 884744 | tf_op jit(solution)/shard_map/ppermute | solution.py:289

commit v5 on v4

--- a/solution.py
+++ b/solution.py
@@ -11,6 +11,8 @@
 BLOCK = 128
 ROOM = 24 * 1024 * 1024
 HIGHEST = lax.Precision.HIGHEST
+PANEL = 8
+NEAR = 1e-5
 F32 = jnp.float32
 BF16 = jnp.bfloat16
 NT = (((1,), (1,)), ((), ()))
@@ -28,6 +30,11 @@
     middle = rest.astype(BF16)
     low = (rest - middle.astype(F32)).astype(BF16)
     return high, middle, low
+
+
+def split2(x):
+    high = x.astype(BF16)
+    return high, (x - high.astype(F32)).astype(BF16)
 
 
 def layout(n):
@@ -45,27 +52,31 @@
     return list(zip(edges[:-1], edges[1:]))
 
 
-def gram_kernel(plan, core_of, features, keep, send, held, arrived):
+def gram_kernel(plan, core_of, features, keep, send, held, top, bottom, arrived):
     width = features.shape[1]
     n = width // BLOCK
     half = width // 2
     copies = []
     for k, (start, stop) in enumerate(plan):
         rows = pl.ds(start, stop - start)
-        copies.append(pltpu.make_async_copy(features.at[rows], held.at[rows], arrived.at[k]))
-    for copy in copies[:2]:
+        copy = pltpu.make_async_copy(features.at[rows], held.at[rows], arrived.at[k])
         copy.start()
+        copies.append(copy)
     core = core_of()
-    top = bottom = None
-    for k, (start, stop) in enumerate(plan):
+
+    def add(k):
+        start, stop = plan[k]
         copies[k].wait()
-        if k + 2 < len(copies):
-            copies[k + 2].start()
         f = held[start:stop, :]
         a = dot(f[:, :half], f, TN)
         b = dot(f[:, half:], f[:, half:], TN)
-        top = a if top is None else top + a
-        bottom = b if bottom is None else bottom + b
+        top[...] = top[...] + a if k else a
+        bottom[...] = bottom[...] + b if k else b
+
+    for k in range(len(plan) - 1):
+        pl.when(core >= 0)(functools.partial(add, k))
+    add(len(plan) - 1)
+
     def block(i, j):
         if i >= n // 2:
             src, i, j = bottom, i - n // 2, j - n // 2
@@ -91,7 +102,7 @@
         at += zero.shape[0]
 
 
-def local_gram(features, core_of, weights=(1, 1)):
+def local_gram(features, core_of, weights=(1, 2)):
     rows, width = features.shape
     n = width // BLOCK
     half = jax.ShapeDtypeStruct((n * (2 * n + 1) * BLOCK // 8, BLOCK), F32)
@@ -103,6 +114,8 @@
         out_specs=(pl.BlockSpec(memory_space=pltpu.VMEM),) * 2,
         scratch_shapes=[
             pltpu.VMEM((rows, width), BF16),
+            pltpu.VMEM((width // 2, width), F32),
+            pltpu.VMEM((width // 2, width // 2), F32),
             pltpu.SemaphoreType.DMA((len(plan),)),
         ],
         compiler_params=pltpu.CompilerParams(vmem_limit_bytes=ROOM),
@@ -127,16 +140,16 @@
 def eliminate(tables, outs):
     rank, width = tables[0].shape
     rests = list(tables)
-    for p in range(0, rank, 8):
+    for p in range(0, rank, PANEL):
         high = rank - p
         panels = [
             [
                 jnp.broadcast_to(rest[:, rank + p + j : rank + p + j + 1], (high, width))
-                for j in range(8)
+                for j in range(PANEL)
             ]
             for rest in rests
         ]
-        for j in range(8):
+        for j in range(PANEL):
             for t, out in enumerate(outs):
                 columns, rest = panels[t], rests[t]
                 column = columns[j]
@@ -144,13 +157,30 @@
                 inverse = 1.0 / pivot
                 row = rest[j : j + 1, :]
                 out[p + j : p + j + 1, :] = row * lax.rsqrt(pivot)
-                for i in range(j + 1, 8):
+                for i in range(j + 1, PANEL):
                     columns[i] = columns[i] - column * (columns[i][j : j + 1, :] * inverse)
                 rests[t] = rest - column * (row * inverse)
-        rests = [rest[8:, :] for rest in rests]
-
-
-def nearly_identity(rows):
+        rests = [rest[PANEL:, :] for rest in rests]
+
+
+def eliminate_slowly(gram, table, out):
+    rank, width = gram.shape
+    table[...] = gram
+    lane = lax.broadcasted_iota(jnp.int32, (rank, width), 1)
+
+    def step(k, carry):
+        rest = table[...]
+        column = jnp.sum(jnp.where(lane == rank + k, rest, 0.0), axis=1, keepdims=True)
+        row = table[pl.ds(k, 1), :]
+        pivot = jnp.sum(jnp.where(lane[:1] == rank + k, row, 0.0), axis=1, keepdims=True)
+        out[pl.ds(k, 1), :] = row * lax.rsqrt(pivot)
+        table[...] = rest - column * (row * (1.0 / pivot))
+        return carry
+
+    lax.fori_loop(0, rank, step, 0)
+
+
+def polish(rows):
     rank = rows.shape[0]
     lane = lax.broadcasted_iota(jnp.int32, (rank, rank), 1)
     row = lax.broadcasted_iota(jnp.int32, (rank, rank), 0)
@@ -158,9 +188,11 @@
     half = jnp.where(lane < row, 1.0, 0.0) + 0.5 * eye
     off = dot(rows, rows, NT, HIGHEST) - eye
     first = off * half
-    square = dot(first, first, NN, HIGHEST)
-    outer = dot(first, first, NT, HIGHEST) * half
-    return jnp.sum(off * off), eye + ((square + outer) - first)
+    rough = first.astype(BF16)
+    change = (dot(rough, rough) + dot(rough, rough, NT) * half) - first
+    high, low = split2(change)
+    top, rest = split2(rows)
+    return jnp.sum(off * off), rows + ((dot(low, top) + dot(high, rest)) + dot(high, top))
 
 
 def finish_kernel(
@@ -207,44 +239,64 @@
         eliminate([gram_of(rows, rows)], [table])
         return dot(table[:, :rank], rows, NN, HIGHEST)
 
-    wide = sweep(times_gram(sketch[...]))
-    distance, inverse = nearly_identity(wide)
-    hold[...] = dot(inverse, wide, NN, HIGHEST)
-
-    @pl.when(jnp.logical_not(distance <= 1e-5))
-    def _():
-        hold[...] = sweep(wide)
-
-    estimate = hold[...].astype(BF16)
+    def scale_left(factor, near):
+        for k, part in enumerate(split2(dot(factor, near, NN, HIGHEST) * scale)):
+            weights[k * rank : (k + 1) * rank, :] = part
+
+    raw = times_gram(sketch[...])
+    wide = sweep(raw)
+    distance, polished = polish(wide)
+    estimate = polished.astype(BF16)
     near = estimate.astype(F32)
     image = times_gram(estimate)
     eliminate([gram_of(image, near), gram_of(image, image)], [table, image_table])
-    factor = table[:, :rank]
-    for k, part in enumerate(split3(dot(factor, near, NN, HIGHEST) * scale)):
-        weights[k * rank : (k + 1) * rank, :] = part
+    scale_left(table[:, :rank], near)
     swept = dot(image_table[:, :rank], image, NN, HIGHEST)
-    distance, inverse = nearly_identity(swept)
-    hold[...] = dot(inverse, swept, NN, HIGHEST)
-
-    @pl.when(jnp.logical_not(distance <= 1e-5))
+    distance_too, polished = polish(swept)
+    hold[...] = polished
+
+    @pl.when(jnp.logical_not(distance + distance_too <= NEAR))
     def _():
-        hold[...] = sweep(sweep(dot(factor, image, NN, HIGHEST)))
+        def slow_sweep(rows):
+            eliminate_slowly(gram_of(rows, rows), image_table, table)
+            return dot(table[:, :rank], rows, NN, HIGHEST)
+
+        estimate = slow_sweep(wide).astype(BF16)
+        near = estimate.astype(F32)
+        image = times_gram(estimate)
+        eliminate_slowly(gram_of(image, near), image_table, table)
+        factor = table[:, :rank]
+        scale_left(factor, near)
+        hold[...] = dot(factor, image, NN, HIGHEST)
+
+        def again(k, carry):
+            hold[...] = slow_sweep(hold[...])
+            return carry
+
+        lax.fori_loop(0, 2, again, 0)
 
     basis[...] = hold[...]
-    weights[3 * rank : 4 * rank, :] = hold[...].astype(BF16)
+    weights[2 * rank : 3 * rank, :] = hold[...].astype(BF16)
 
     sends = []
     for k, (start, stop) in enumerate(plan):
-        fetches[k].wait()
-        columns = slice(start, stop)
-        out = dot(weights[...], held[start:stop, :], NT)
-        left_held[:, columns] = (out[2 * rank : 3 * rank] + out[rank : 2 * rank]) + out[:rank]
-        codes_held[:, columns] = out[3 * rank :].astype(BF16)
         span = pl.ds(start, stop - start)
-        for q, (source, target) in enumerate(((left_held, left), (codes_held, codes))):
-            copy = pltpu.make_async_copy(source.at[:, span], target.at[:, span], gone.at[q, k])
-            copy.start()
-            sends.append(copy)
+        own = [
+            pltpu.make_async_copy(source.at[:, span], target.at[:, span], gone.at[q, k])
+            for q, (source, target) in enumerate(((left_held, left), (codes_held, codes)))
+        ]
+        sends += own
+
+        def piece(k=k, start=start, stop=stop, own=own):
+            fetches[k].wait()
+            columns = slice(start, stop)
+            out = dot(weights[...], held[start:stop, :], NT)
+            left_held[:, columns] = out[rank : 2 * rank] + out[:rank]
+            codes_held[:, columns] = out[2 * rank :].astype(BF16)
+            for copy in own:
+                copy.start()
+
+        pl.when(core >= 0)(piece)
     for copy in sends:
         copy.wait()
 
@@ -269,7 +321,7 @@
             pltpu.VMEM((rank, 2 * rank), F32),
             pltpu.VMEM((rank, 2 * rank), F32),
             pltpu.VMEM((rank, width), F32),
-            pltpu.VMEM((4 * rank, width), BF16),
+            pltpu.VMEM((3 * rank, width), BF16),
             pltpu.VMEM((rows, width), BF16),
             pltpu.VMEM((rank, rows), F32),
             pltpu.VMEM((rank, rows), BF16),

time: 82.5 us -> 81.5 us (0.988)
  no operation moved by 1% of the time
where the time goes in v5:
time: 81.5 us; the launch traced here: 81.3 us
  blocking collectives  49.4 us (61%)
  starting transfers between devices  15.4 us (19%)
  Pallas kernels  13 us (16%)
  waiting for transfers between devices  2.37 us (3%)
    all_to_all x3, blocking collectives, exchange(): return lax.all_to_all(parts, axes, split_axis=0, concat_axis=0, tiled=True)  49.4 us
    ppermute x2, starting transfers between devices, swap(): return lax.ppermute(x, 'c', [(0, 1), (1, 0)])  15.4 us
    pallas_call x1, Pallas kernels, finish(): pl.pallas_call(functools.partial(finish_kernel, scale, plan, core_of), ou...  9.76 us
    pallas_call x1, Pallas kernels, local_gram(): pl.pallas_call(functools.partial(gram_kernel, plan, core_of), out_shape=(...  3.2 us
    ppermute x2, waiting for transfers between devices, swap(): return lax.ppermute(x, 'c', [(0, 1), (1, 0)])  2.37 us
  transfers between devices with their start and end apart: 2, of which 2 were waited for; matrix products, arithmetic and copies ran while one was open for 0% of the time, Pallas kernels for 0%

profile of v5, /device:TPU:1, one launch (start us, length us, event | category | flops | bytes accessed | tf_op | source)
XLA Modules:
  0.0 81.3 jit_solution(8407203309645113868)
XLA Ops:
  0.6 0.0 copy-start
  0.6 3.2 %gram.1 = (f32[576,128]{1,0:T(8,128)S(1)}, f32[576,128]{1,0:T(8,128)S(1)}) custom-call(bf16[3328,512]{1,0:T(8,128)(2,1)} %features.3), custom_call_target="tpu_custom_call" | custom-call | flops 1744830464 | bytes 3407872 | tf_op jit(solution)/shard_map/gram/pallas_call | solution.py:110
  3.9 8.8 %collective-permute-start = (f32[576,128]{1,0:T(8,128)S(1)}, f32[576,128]{1,0:T(8,128)S(1)}, u32[]{:S(2)}, u32[]{:S(2)}) collective-permute-start(f32[576,128]{1,0:T(8,128)S(1)} %get-tuple-element.9), channel_id=1, source_target_pairs={{0,1},{1,0},{2,3},{3,2},{4,5},{5,4},{6,7},{7,6},{8,9},{9,8},{10,11... | collective-permute-start | bytes 884744 | tf_op jit(solution)/shard_map/ppermute | solution.py:341
  12.6 1.2 %collective-permute-done = f32[576,128]{1,0:T(8,128)S(1)} collective-permute-done((f32[576,128]{1,0:T(8,128)S(1)}, f32[576,128]{1,0:T(8,128)S(1)}, u32[]{:S(2)}, u32[]{:S(2)}) %collective-permute-start) | collective-permute-done | bytes 294944 | tf_op jit(solution)/shard_map/ppermute | solution.py:341
  13.9 12.2 %all_to_all.15 = f32[32,18,1,128]{3,2,1,0:T(1,128)S(1)} all-to-all(f32[32,18,1,128]{3,2,1,0:T(1,128)S(1)} %bitcast.9), channel_id=1, replica_groups=mesh['gx'=16,'far'=8,'near'=2,'c'=2] {'gx','near'}, dimensions={0} | all-to-all | bytes 589824 | tf_op jit(solution)/shard_map/all_to_all | solution.py:337
  26.1 0.2 reduce_sum.18
  26.3 25.4 %all_to_all.16 = f32[8,18,1,128]{3,2,1,0:T(1,128)S(1)} all-to-all(f32[8,18,1,128]{3,2,1,0:T(1,128)S(1)} %broadcast_in_dim.6), channel_id=1, replica_groups=mesh['gx'=16,'far'=8,'near'=2,'c'=2] {'far'}, dimensions={0} | all-to-all | bytes 147456 | tf_op jit(solution)/shard_map/all_to_all | solution.py:337
  51.8 0.1 reduce_sum.19
  51.8 0.2 broadcast_in_dim.7
  52.0 11.7 %all_to_all.17 = f32[32,18,1,128]{3,2,1,0:T(1,128)S(1)} all-to-all(f32[32,18,1,128]{3,2,1,0:T(1,128)S(1)} %broadcast_in_dim.7), channel_id=1, replica_groups=mesh['gx'=16,'far'=8,'near'=2,'c'=2] {'gx','near'}, dimensions={0} | all-to-all | bytes 589824 | tf_op jit(solution)/shard_map/all_to_all | solution.py:337
  63.7 6.6 %collective-permute-start.1 = (f32[576,128]{1,0:T(8,128)S(1)}, f32[576,128]{1,0:T(8,128)S(1)}, u32[]{:S(2)}, u32[]{:S(2)}) collective-permute-start(f32[576,128]{1,0:T(8,128)S(1)} %bitcast.6), channel_id=1, source_target_pairs={{0,1},{1,0},{2,3},{3,2},{4,5},{5,4},{6,7},{7,6},{8,9},{9,8},{10,11... | collective-permute-start | bytes 884744 | tf_op jit(solution)/shard_map/ppermute | solution.py:341
  70.3 1.2 %collective-permute-done.1.other = f32[576,128]{1,0:T(8,128)S(1)} collective-permute-done((f32[576,128]{1,0:T(8,128)S(1)}, f32[576,128]{1,0:T(8,128)S(1)}, u32[]{:S(2)}, u32[]{:S(2)}) %collective-permute-start.1) | collective-permute-done | bytes 294944 | tf_op jit(solution)/shard_map/ppermute | solution.py:341
  71.5 0.0 copy-done
  71.5 9.8 %finish.1 = (f32[64,512]{1,0:T(8,128)}, f32[64,3328]{1,0:T(8,128)}, bf16[64,3328]{1,0:T(8,128)(2,1)}) custom-call(f32[576,128]{1,0:T(8,128)S(1)} %bitcast.7, f32[576,128]{1,0:T(8,128)S(1)} %collective-permute-done.1.other, bf16[64,512]{1,0:T(8,128)(2,1)S(1)} %bitcast.8, bf16[3328,512]{1,0:T(8,128)(2,1)} %features.3), custom_call_target="tpu_custom_call" | custom-call | tf_op jit(solution)/shard_map/finish/pallas_call | solution.py:310
  (2 shorter events, 0.1 us)
Async XLA Ops:
  0.6 70.9 %copy-start = (bf16[512,64]{0,1:T(8,128)(2,1)S(1)}, bf16[512,64]{0,1:T(8,128)(2,1)}, u32[]{:S(2)}) copy-start(bf16[512,64]{0,1:T(8,128)(2,1)} %param.3) | copy-start | bytes 196612
  3.9 10.0 %collective-permute-start = (f32[576,128]{1,0:T(8,128)S(1)}, f32[576,128]{1,0:T(8,128)S(1)}, u32[]{:S(2)}, u32[]{:S(2)}) collective-permute-start(f32[576,128]{1,0:T(8,128)S(1)} %get-tuple-element.9), channel_id=1, source_target_pairs={{0,1},{1,0},{2,3},{3,2},{4,5},{5,4},{6,7},{7,6},{8,9},{9,8},{10,11... | collective-permute-start | bytes 884744 | tf_op jit(solution)/shard_map/ppermute | solution.py:341
  63.7 7.8 %collective-permute-start.1 = (f32[576,128]{1,0:T(8,128)S(1)}, f32[576,128]{1,0:T(8,128)S(1)}, u32[]{:S(2)}, u32[]{:S(2)}) collective-permute-start(f32[576,128]{1,0:T(8,128)S(1)} %bitcast.6), channel_id=1, source_target_pairs={{0,1},{1,0},{2,3},{3,2},{4,5},{5,4},{6,7},{7,6},{8,9},{9,8},{10,11... | collective-permute-start | bytes 884744 | tf_op jit(solution)/shard_map/ppermute | solution.py:341

commit v6 on v5

--- a/solution.py
+++ b/solution.py
@@ -11,7 +11,6 @@
 BLOCK = 128
 ROOM = 24 * 1024 * 1024
 HIGHEST = lax.Precision.HIGHEST
-PANEL = 8
 NEAR = 1e-5
 F32 = jnp.float32
 BF16 = jnp.bfloat16
@@ -140,16 +139,19 @@
 def eliminate(tables, outs):
     rank, width = tables[0].shape
     rests = list(tables)
-    for p in range(0, rank, PANEL):
-        high = rank - p
-        panels = [
-            [
-                jnp.broadcast_to(rest[:, rank + p + j : rank + p + j + 1], (high, width))
-                for j in range(PANEL)
-            ]
-            for rest in rests
+
+    def spread(rest, skip, at):
+        high = rest.shape[0] - skip
+        return [
+            jnp.broadcast_to(rest[skip:, at + j : at + j + 1], (high, width)) for j in range(8)
         ]
-        for j in range(PANEL):
+
+    panels = [spread(rest, 0, rank) for rest in rests]
+    for p in range(0, rank, 8):
+        last = p + 8 == rank
+        look = len(outs) == 1
+        ahead = [[] if last or not look else spread(rest, 8, rank + p + 8) for rest in rests]
+        for j in range(8):
             for t, out in enumerate(outs):
                 columns, rest = panels[t], rests[t]
                 column = columns[j]
@@ -157,10 +159,15 @@
                 inverse = 1.0 / pivot
                 row = rest[j : j + 1, :]
                 out[p + j : p + j + 1, :] = row * lax.rsqrt(pivot)
-                for i in range(j + 1, PANEL):
-                    columns[i] = columns[i] - column * (columns[i][j : j + 1, :] * inverse)
+                for i in range(j + 1, 8):
+                    columns[i] = columns[i] - column * (column[i : i + 1, :] * inverse)
+                for i in range(len(ahead[t])):
+                    factor = column[8 + i : 9 + i, :] * inverse
+                    ahead[t][i] = ahead[t][i] - column[8:, :] * factor
                 rests[t] = rest - column * (row * inverse)
-        rests = [rest[PANEL:, :] for rest in rests]
+        rests = [rest[8:, :] for rest in rests]
+        if not last:
+            panels = ahead if look else [spread(rest, 0, rank + p + 8) for rest in rests]
 
 
 def eliminate_slowly(gram, table, out):
@@ -197,7 +204,7 @@
 
 def finish_kernel(
     scale, plan, core_of, mine, other, sketch, features, basis, left, codes,
-    parts, table, image_table, hold, weights, held, left_held, codes_held, arrived, gone,
+    parts, table, image_table, hold, weights, held, left_held, codes_held, arrived, gone, done,
 ):
     rank, width = sketch.shape
     n = width // BLOCK
@@ -275,10 +282,11 @@
 
         lax.fori_loop(0, 2, again, 0)
 
-    basis[...] = hold[...]
+    own_copy = pltpu.make_async_copy(hold, basis, done)
+    own_copy.start()
     weights[2 * rank : 3 * rank, :] = hold[...].astype(BF16)
 
-    sends = []
+    sends = [own_copy]
     for k, (start, stop) in enumerate(plan):
         span = pl.ds(start, stop - start)
         own = [
@@ -315,7 +323,7 @@
             jax.ShapeDtypeStruct((rank, rows), BF16),
         ),
         in_specs=[vmem, vmem, vmem, hbm],
-        out_specs=(vmem, hbm, hbm),
+        out_specs=(hbm, hbm, hbm),
         scratch_shapes=[
             pltpu.VMEM((3, width, width), BF16),
             pltpu.VMEM((rank, 2 * rank), F32),
@@ -327,6 +335,7 @@
             pltpu.VMEM((rank, rows), BF16),
             pltpu.SemaphoreType.DMA((len(plan),)),
             pltpu.SemaphoreType.DMA((2, len(plan))),
+            pltpu.SemaphoreType.DMA(()),
         ],
         compiler_params=pltpu.CompilerParams(vmem_limit_bytes=ROOM),
         name="finish",

time: 81.5 us -> 80.8 us (level)
  no operation moved by 1% of the time
where the time goes in v6:
time: 80.8 us; the launch traced here: 80.5 us
  blocking collectives  49.4 us (61%)
  starting transfers between devices  15.4 us (19%)
  Pallas kernels  12.2 us (15%)
  waiting for transfers between devices  2.37 us (3%)
    all_to_all x3, blocking collectives, exchange(): return lax.all_to_all(parts, axes, split_axis=0, concat_axis=0, tiled=True)  49.4 us
    ppermute x2, starting transfers between devices, swap(): return lax.ppermute(x, 'c', [(0, 1), (1, 0)])  15.4 us
    pallas_call x1, Pallas kernels, finish(): pl.pallas_call(functools.partial(finish_kernel, scale, plan, core_of), ou...  8.99 us
    pallas_call x1, Pallas kernels, local_gram(): pl.pallas_call(functools.partial(gram_kernel, plan, core_of), out_shape=(...  3.2 us
    ppermute x2, waiting for transfers between devices, swap(): return lax.ppermute(x, 'c', [(0, 1), (1, 0)])  2.37 us
  transfers between devices with their start and end apart: 2, of which 2 were waited for; matrix products, arithmetic and copies ran while one was open for 0% of the time, Pallas kernels for 0%

profile of v6, /device:TPU:1, one launch (start us, length us, event | category | flops | bytes accessed | tf_op | source)
XLA Modules:
  0.0 80.5 jit_solution(17379531552124091723)
XLA Ops:
  0.6 0.0 copy-start
  0.6 3.2 %gram.1 = (f32[576,128]{1,0:T(8,128)S(1)}, f32[576,128]{1,0:T(8,128)S(1)}) custom-call(bf16[3328,512]{1,0:T(8,128)(2,1)} %features.3), custom_call_target="tpu_custom_call" | custom-call | flops 1744830464 | bytes 3407872 | tf_op jit(solution)/shard_map/gram/pallas_call | solution.py:109
  3.9 8.8 %collective-permute-start = (f32[576,128]{1,0:T(8,128)S(1)}, f32[576,128]{1,0:T(8,128)S(1)}, u32[]{:S(2)}, u32[]{:S(2)}) collective-permute-start(f32[576,128]{1,0:T(8,128)S(1)} %get-tuple-element.9), channel_id=1, source_target_pairs={{0,1},{1,0},{2,3},{3,2},{4,5},{5,4},{6,7},{7,6},{8,9},{9,8},{10,11... | collective-permute-start | bytes 884744 | tf_op jit(solution)/shard_map/ppermute | solution.py:350
  12.6 1.2 %collective-permute-done = f32[576,128]{1,0:T(8,128)S(1)} collective-permute-done((f32[576,128]{1,0:T(8,128)S(1)}, f32[576,128]{1,0:T(8,128)S(1)}, u32[]{:S(2)}, u32[]{:S(2)}) %collective-permute-start) | collective-permute-done | bytes 294944 | tf_op jit(solution)/shard_map/ppermute | solution.py:350
  13.9 12.2 %all_to_all.15 = f32[32,18,1,128]{3,2,1,0:T(1,128)S(1)} all-to-all(f32[32,18,1,128]{3,2,1,0:T(1,128)S(1)} %bitcast.9), channel_id=1, replica_groups=mesh['gx'=16,'far'=8,'near'=2,'c'=2] {'gx','near'}, dimensions={0} | all-to-all | bytes 589824 | tf_op jit(solution)/shard_map/all_to_all | solution.py:346
  26.1 0.2 reduce_sum.18
  26.3 25.4 %all_to_all.16 = f32[8,18,1,128]{3,2,1,0:T(1,128)S(1)} all-to-all(f32[8,18,1,128]{3,2,1,0:T(1,128)S(1)} %broadcast_in_dim.6), channel_id=1, replica_groups=mesh['gx'=16,'far'=8,'near'=2,'c'=2] {'far'}, dimensions={0} | all-to-all | bytes 147456 | tf_op jit(solution)/shard_map/all_to_all | solution.py:346
  51.8 0.1 reduce_sum.19
  51.8 0.2 broadcast_in_dim.7
  52.0 11.7 %all_to_all.17 = f32[32,18,1,128]{3,2,1,0:T(1,128)S(1)} all-to-all(f32[32,18,1,128]{3,2,1,0:T(1,128)S(1)} %broadcast_in_dim.7), channel_id=1, replica_groups=mesh['gx'=16,'far'=8,'near'=2,'c'=2] {'gx','near'}, dimensions={0} | all-to-all | bytes 589824 | tf_op jit(solution)/shard_map/all_to_all | solution.py:346
  63.7 6.6 %collective-permute-start.1 = (f32[576,128]{1,0:T(8,128)S(1)}, f32[576,128]{1,0:T(8,128)S(1)}, u32[]{:S(2)}, u32[]{:S(2)}) collective-permute-start(f32[576,128]{1,0:T(8,128)S(1)} %bitcast.6), channel_id=1, source_target_pairs={{0,1},{1,0},{2,3},{3,2},{4,5},{5,4},{6,7},{7,6},{8,9},{9,8},{10,11... | collective-permute-start | bytes 884744 | tf_op jit(solution)/shard_map/ppermute | solution.py:350
  70.3 1.2 %collective-permute-done.1.other = f32[576,128]{1,0:T(8,128)S(1)} collective-permute-done((f32[576,128]{1,0:T(8,128)S(1)}, f32[576,128]{1,0:T(8,128)S(1)}, u32[]{:S(2)}, u32[]{:S(2)}) %collective-permute-start.1) | collective-permute-done | bytes 294944 | tf_op jit(solution)/shard_map/ppermute | solution.py:350
  71.5 0.0 copy-done
  71.5 9.0 %finish.1 = (f32[64,512]{1,0:T(8,128)}, f32[64,3328]{1,0:T(8,128)}, bf16[64,3328]{1,0:T(8,128)(2,1)}) custom-call(f32[576,128]{1,0:T(8,128)S(1)} %bitcast.7, f32[576,128]{1,0:T(8,128)S(1)} %collective-permute-done.1.other, bf16[64,512]{1,0:T(8,128)(2,1)S(1)} %bitcast.8, bf16[3328,512]{1,0:T(8,128)(2,1)} %features.3), custom_call_target="tpu_custom_call" | custom-call | tf_op jit(solution)/shard_map/finish/pallas_call | solution.py:318
  (2 shorter events, 0.1 us)
Async XLA Ops:
  0.6 70.9 %copy-start = (bf16[512,64]{0,1:T(8,128)(2,1)S(1)}, bf16[512,64]{0,1:T(8,128)(2,1)}, u32[]{:S(2)}) copy-start(bf16[512,64]{0,1:T(8,128)(2,1)} %param.3) | copy-start | bytes 196612
  3.9 10.0 %collective-permute-start = (f32[576,128]{1,0:T(8,128)S(1)}, f32[576,128]{1,0:T(8,128)S(1)}, u32[]{:S(2)}, u32[]{:S(2)}) collective-permute-start(f32[576,128]{1,0:T(8,128)S(1)} %get-tuple-element.9), channel_id=1, source_target_pairs={{0,1},{1,0},{2,3},{3,2},{4,5},{5,4},{6,7},{7,6},{8,9},{9,8},{10,11... | collective-permute-start | bytes 884744 | tf_op jit(solution)/shard_map/ppermute | solution.py:350
  63.7 7.8 %collective-permute-start.1 = (f32[576,128]{1,0:T(8,128)S(1)}, f32[576,128]{1,0:T(8,128)S(1)}, u32[]{:S(2)}, u32[]{:S(2)}) collective-permute-start(f32[576,128]{1,0:T(8,128)S(1)} %bitcast.6), channel_id=1, source_target_pairs={{0,1},{1,0},{2,3},{3,2},{4,5},{5,4},{6,7},{7,6},{8,9},{9,8},{10,11... | collective-permute-start | bytes 884744 | tf_op jit(solution)/shard_map/ppermute | solution.py:350

commit v7 on v6

--- a/solution.py
+++ b/solution.py
@@ -355,7 +355,8 @@
     cells, length = lax.axis_size(slab), lax.axis_size(line)
     half = keep + swap(send)
     rows, width = half.shape
-    share = jnp.sum(exchange(half.reshape(cells, rows // cells, 1, width), slab), axis=0)
+    pieces = half.reshape(cells, rows // cells // 2, 2, width)
+    share = jnp.sum(exchange(pieces, slab), axis=0)
     share = jnp.sum(exchange(jnp.broadcast_to(share, (length, *share.shape)), line), axis=0)
     mine = exchange(jnp.broadcast_to(share, (cells, *share.shape)), slab).reshape(rows, width)
     return mine, swap(mine)

time: 80.8 us -> 80.6 us (level)
  no operation moved by 1% of the time
where the time goes in v7:
time: 80.6 us; the launch traced here: 80.3 us
  blocking collectives  49.4 us (61%)
  starting transfers between devices  15.4 us (19%)
  Pallas kernels  12.2 us (15%)
  waiting for transfers between devices  2.37 us (3%)
    all_to_all x3, blocking collectives, exchange(): return lax.all_to_all(parts, axes, split_axis=0, concat_axis=0, tiled=True)  49.4 us
    ppermute x2, starting transfers between devices, swap(): return lax.ppermute(x, 'c', [(0, 1), (1, 0)])  15.4 us
    pallas_call x1, Pallas kernels, finish(): pl.pallas_call(functools.partial(finish_kernel, scale, plan, core_of), ou...  8.99 us
    pallas_call x1, Pallas kernels, local_gram(): pl.pallas_call(functools.partial(gram_kernel, plan, core_of), out_shape=(...  3.2 us
    ppermute x2, waiting for transfers between devices, swap(): return lax.ppermute(x, 'c', [(0, 1), (1, 0)])  2.37 us
  transfers between devices with their start and end apart: 2, of which 2 were waited for; matrix products, arithmetic and copies ran while one was open for 0% of the time, Pallas kernels for 0%

profile of v7, /device:TPU:1, one launch (start us, length us, event | category | flops | bytes accessed | tf_op | source)
XLA Modules:
  0.0 80.3 jit_solution(14187986654026059948)
XLA Ops:
  0.6 0.0 copy-start
  0.6 3.2 %gram.1 = (f32[576,128]{1,0:T(8,128)S(1)}, f32[576,128]{1,0:T(8,128)S(1)}) custom-call(bf16[3328,512]{1,0:T(8,128)(2,1)} %features.3), custom_call_target="tpu_custom_call" | custom-call | flops 1744830464 | bytes 3407872 | tf_op jit(solution)/shard_map/gram/pallas_call | solution.py:109
  3.9 8.8 %collective-permute-start = (f32[576,128]{1,0:T(8,128)S(1)}, f32[576,128]{1,0:T(8,128)S(1)}, u32[]{:S(2)}, u32[]{:S(2)}) collective-permute-start(f32[576,128]{1,0:T(8,128)S(1)} %get-tuple-element.9), channel_id=1, source_target_pairs={{0,1},{1,0},{2,3},{3,2},{4,5},{5,4},{6,7},{7,6},{8,9},{9,8},{10,11... | collective-permute-start | bytes 884744 | tf_op jit(solution)/shard_map/ppermute | solution.py:350
  12.6 1.2 %collective-permute-done = f32[576,128]{1,0:T(8,128)S(1)} collective-permute-done((f32[576,128]{1,0:T(8,128)S(1)}, f32[576,128]{1,0:T(8,128)S(1)}, u32[]{:S(2)}, u32[]{:S(2)}) %collective-permute-start) | collective-permute-done | bytes 294944 | tf_op jit(solution)/shard_map/ppermute | solution.py:350
  13.9 12.2 %all_to_all.15 = f32[32,9,2,128]{3,2,1,0:T(2,128)S(1)} all-to-all(f32[32,9,2,128]{3,2,1,0:T(2,128)S(1)} %bitcast.9), channel_id=1, replica_groups=mesh['gx'=16,'far'=8,'near'=2,'c'=2] {'gx','near'}, dimensions={0} | all-to-all | bytes 589824 | tf_op jit(solution)/shard_map/all_to_all | solution.py:346
  26.1 0.1 reduce_sum.18
  26.2 25.4 %all_to_all.16 = f32[8,9,2,128]{3,2,1,0:T(2,128)S(1)} all-to-all(f32[8,9,2,128]{3,2,1,0:T(2,128)S(1)} %broadcast_in_dim.6), channel_id=1, replica_groups=mesh['gx'=16,'far'=8,'near'=2,'c'=2] {'far'}, dimensions={0} | all-to-all | bytes 147456 | tf_op jit(solution)/shard_map/all_to_all | solution.py:346
  51.7 0.1 broadcast_in_dim.7
  51.8 11.7 %all_to_all.17 = f32[32,9,2,128]{3,2,1,0:T(2,128)S(1)} all-to-all(f32[32,9,2,128]{3,2,1,0:T(2,128)S(1)} %broadcast_in_dim.7), channel_id=1, replica_groups=mesh['gx'=16,'far'=8,'near'=2,'c'=2] {'gx','near'}, dimensions={0} | all-to-all | bytes 589824 | tf_op jit(solution)/shard_map/all_to_all | solution.py:346
  63.5 6.6 %collective-permute-start.1 = (f32[576,128]{1,0:T(8,128)S(1)}, f32[576,128]{1,0:T(8,128)S(1)}, u32[]{:S(2)}, u32[]{:S(2)}) collective-permute-start(f32[576,128]{1,0:T(8,128)S(1)} %bitcast.6), channel_id=1, source_target_pairs={{0,1},{1,0},{2,3},{3,2},{4,5},{5,4},{6,7},{7,6},{8,9},{9,8},{10,11... | collective-permute-start | bytes 884744 | tf_op jit(solution)/shard_map/ppermute | solution.py:350
  70.1 1.2 %collective-permute-done.1.other = f32[576,128]{1,0:T(8,128)S(1)} collective-permute-done((f32[576,128]{1,0:T(8,128)S(1)}, f32[576,128]{1,0:T(8,128)S(1)}, u32[]{:S(2)}, u32[]{:S(2)}) %collective-permute-start.1) | collective-permute-done | bytes 294944 | tf_op jit(solution)/shard_map/ppermute | solution.py:350
  71.3 0.0 copy-done
  71.3 9.0 %finish.1 = (f32[64,512]{1,0:T(8,128)}, f32[64,3328]{1,0:T(8,128)}, bf16[64,3328]{1,0:T(8,128)(2,1)}) custom-call(f32[576,128]{1,0:T(8,128)S(1)} %bitcast.7, f32[576,128]{1,0:T(8,128)S(1)} %collective-permute-done.1.other, bf16[64,512]{1,0:T(8,128)(2,1)S(1)} %bitcast.8, bf16[3328,512]{1,0:T(8,128)(2,1)} %features.3), custom_call_target="tpu_custom_call" | custom-call | tf_op jit(solution)/shard_map/finish/pallas_call | solution.py:318
  (3 shorter events, 0.1 us)
Async XLA Ops:
  0.6 70.7 %copy-start = (bf16[512,64]{0,1:T(8,128)(2,1)S(1)}, bf16[512,64]{0,1:T(8,128)(2,1)}, u32[]{:S(2)}) copy-start(bf16[512,64]{0,1:T(8,128)(2,1)} %param.3) | copy-start | bytes 196612
  3.9 10.0 %collective-permute-start = (f32[576,128]{1,0:T(8,128)S(1)}, f32[576,128]{1,0:T(8,128)S(1)}, u32[]{:S(2)}, u32[]{:S(2)}) collective-permute-start(f32[576,128]{1,0:T(8,128)S(1)} %get-tuple-element.9), channel_id=1, source_target_pairs={{0,1},{1,0},{2,3},{3,2},{4,5},{5,4},{6,7},{7,6},{8,9},{9,8},{10,11... | collective-permute-start | bytes 884744 | tf_op jit(solution)/shard_map/ppermute | solution.py:350
  63.5 7.8 %collective-permute-start.1 = (f32[576,128]{1,0:T(8,128)S(1)}, f32[576,128]{1,0:T(8,128)S(1)}, u32[]{:S(2)}, u32[]{:S(2)}) collective-permute-start(f32[576,128]{1,0:T(8,128)S(1)} %bitcast.6), channel_id=1, source_target_pairs={{0,1},{1,0},{2,3},{3,2},{4,5},{5,4},{6,7},{7,6},{8,9},{9,8},{10,11... | collective-permute-start | bytes 884744 | tf_op jit(solution)/shard_map/ppermute | solution.py:350

commit v8 on v7

--- a/solution.py
+++ b/solution.py
@@ -125,6 +125,14 @@
     )(pltpu.with_memory_space_constraint(features, pltpu.HBM))
 
 
+def stacked(a, b):
+    ah, am, al = split3(a)
+    bh, bm, bl = split3(b)
+    left = jnp.concatenate([al, am, ah, am, ah, ah], axis=1)
+    right = jnp.concatenate([bh, bm, bl, bh, bm, bh], axis=0)
+    return dot(left, right)
+
+
 def beside_identity(gram, rank):
     lane = lax.broadcasted_iota(jnp.int32, (rank, 2 * rank), 1)
     row = lax.broadcasted_iota(jnp.int32, (rank, 2 * rank), 0)
@@ -240,11 +248,12 @@
             store(i, i, jnp.where((row >= BLOCK // 2) & (lane < BLOCK // 2), block.T, block))
 
     def times_gram(rows):
-        return (dot(rows, parts[2]) + dot(rows, parts[1])) + dot(rows, parts[0])
+        deep = parts.shape[0] * width
+        return dot(jnp.concatenate([rows] * 3, axis=1), parts[...].reshape(deep, width))
 
     def sweep(rows):
         eliminate([gram_of(rows, rows)], [table])
-        return dot(table[:, :rank], rows, NN, HIGHEST)
+        return stacked(table[:, :rank], rows)
 
     def scale_left(factor, near):
         for k, part in enumerate(split2(dot(factor, near, NN, HIGHEST) * scale)):
@@ -258,7 +267,7 @@
     image = times_gram(estimate)
     eliminate([gram_of(image, near), gram_of(image, image)], [table, image_table])
     scale_left(table[:, :rank], near)
-    swept = dot(image_table[:, :rank], image, NN, HIGHEST)
+    swept = stacked(image_table[:, :rank], image)
     distance_too, polished = polish(swept)
     hold[...] = polished
 
@@ -351,7 +360,7 @@
 
 
 def sum_everywhere(keep, send):
-    slab, line = ("gx", "near"), "far"
+    slab, line = ("near", "gx"), "far"
     cells, length = lax.axis_size(slab), lax.axis_size(line)
     half = keep + swap(send)
     rows, width = half.shape

time: 80.6 us -> 80.2 us (level)
  no operation moved by 1% of the time
where the time goes in v8:
time: 80.2 us; the launch traced here: 79.9 us
  blocking collectives  48.9 us (61%)
  starting transfers between devices  15.6 us (19%)
  Pallas kernels  12.1 us (15%)
  waiting for transfers between devices  2.37 us (3%)
    all_to_all x3, blocking collectives, exchange(): return lax.all_to_all(parts, axes, split_axis=0, concat_axis=0, tiled=True)  48.9 us
    ppermute x2, starting transfers between devices, swap(): return lax.ppermute(x, 'c', [(0, 1), (1, 0)])  15.6 us
    pallas_call x1, Pallas kernels, finish(): pl.pallas_call(functools.partial(finish_kernel, scale, plan, core_of), ou...  8.93 us
    pallas_call x1, Pallas kernels, local_gram(): pl.pallas_call(functools.partial(gram_kernel, plan, core_of), out_shape=(...  3.2 us
    ppermute x2, waiting for transfers between devices, swap(): return lax.ppermute(x, 'c', [(0, 1), (1, 0)])  2.37 us
  transfers between devices with their start and end apart: 2, of which 2 were waited for; matrix products, arithmetic and copies ran while one was open for 0% of the time, Pallas kernels for 0%

profile of v8, /device:TPU:1, one launch (start us, length us, event | category | flops | bytes accessed | tf_op | source)
XLA Modules:
  0.0 79.9 jit_solution(438497122744969170)
XLA Ops:
  0.6 0.0 copy-start
  0.6 3.2 %gram.1 = (f32[576,128]{1,0:T(8,128)S(1)}, f32[576,128]{1,0:T(8,128)S(1)}) custom-call(bf16[3328,512]{1,0:T(8,128)(2,1)} %features.3), custom_call_target="tpu_custom_call" | custom-call | flops 1744830464 | bytes 3407872 | tf_op jit(solution)/shard_map/gram/pallas_call | solution.py:109
  3.9 8.8 %collective-permute-start = (f32[576,128]{1,0:T(8,128)S(1)}, f32[576,128]{1,0:T(8,128)S(1)}, u32[]{:S(2)}, u32[]{:S(2)}) collective-permute-start(f32[576,128]{1,0:T(8,128)S(1)} %get-tuple-element.9), channel_id=1, source_target_pairs={{0,1},{1,0},{2,3},{3,2},{4,5},{5,4},{6,7},{7,6},{8,9},{9,8},{10,11... | collective-permute-start | bytes 884744 | tf_op jit(solution)/shard_map/ppermute | solution.py:359
  12.6 1.2 %collective-permute-done = f32[576,128]{1,0:T(8,128)S(1)} collective-permute-done((f32[576,128]{1,0:T(8,128)S(1)}, f32[576,128]{1,0:T(8,128)S(1)}, u32[]{:S(2)}, u32[]{:S(2)}) %collective-permute-start) | collective-permute-done | bytes 294944 | tf_op jit(solution)/shard_map/ppermute | solution.py:359
  13.9 11.6 %all_to_all.15 = f32[32,9,2,128]{3,2,1,0:T(2,128)S(1)} all-to-all(f32[32,9,2,128]{3,2,1,0:T(2,128)S(1)} %bitcast.9), channel_id=1, replica_groups=mesh['gx'=16,'far'=8,'near'=2,'c'=2] {'near','gx'}, dimensions={0} | all-to-all | bytes 589824 | tf_op jit(solution)/shard_map/all_to_all | solution.py:355
  25.4 0.1 reduce_sum.18
  25.6 25.7 %all_to_all.16 = f32[8,9,2,128]{3,2,1,0:T(2,128)S(1)} all-to-all(f32[8,9,2,128]{3,2,1,0:T(2,128)S(1)} %broadcast_in_dim.6), channel_id=1, replica_groups=mesh['gx'=16,'far'=8,'near'=2,'c'=2] {'far'}, dimensions={0} | all-to-all | bytes 147456 | tf_op jit(solution)/shard_map/all_to_all | solution.py:355
  51.3 0.1 broadcast_in_dim.7
  51.4 11.6 %all_to_all.17 = f32[32,9,2,128]{3,2,1,0:T(2,128)S(1)} all-to-all(f32[32,9,2,128]{3,2,1,0:T(2,128)S(1)} %broadcast_in_dim.7), channel_id=1, replica_groups=mesh['gx'=16,'far'=8,'near'=2,'c'=2] {'near','gx'}, dimensions={0} | all-to-all | bytes 589824 | tf_op jit(solution)/shard_map/all_to_all | solution.py:355
  63.0 6.8 %collective-permute-start.1 = (f32[576,128]{1,0:T(8,128)S(1)}, f32[576,128]{1,0:T(8,128)S(1)}, u32[]{:S(2)}, u32[]{:S(2)}) collective-permute-start(f32[576,128]{1,0:T(8,128)S(1)} %bitcast.6), channel_id=1, source_target_pairs={{0,1},{1,0},{2,3},{3,2},{4,5},{5,4},{6,7},{7,6},{8,9},{9,8},{10,11... | collective-permute-start | bytes 884744 | tf_op jit(solution)/shard_map/ppermute | solution.py:359
  69.8 1.2 %collective-permute-done.1.other = f32[576,128]{1,0:T(8,128)S(1)} collective-permute-done((f32[576,128]{1,0:T(8,128)S(1)}, f32[576,128]{1,0:T(8,128)S(1)}, u32[]{:S(2)}, u32[]{:S(2)}) %collective-permute-start.1) | collective-permute-done | bytes 294944 | tf_op jit(solution)/shard_map/ppermute | solution.py:359
  71.0 0.0 copy-done
  71.0 8.9 %finish.1 = (f32[64,512]{1,0:T(8,128)}, f32[64,3328]{1,0:T(8,128)}, bf16[64,3328]{1,0:T(8,128)(2,1)}) custom-call(f32[576,128]{1,0:T(8,128)S(1)} %bitcast.7, f32[576,128]{1,0:T(8,128)S(1)} %collective-permute-done.1.other, bf16[64,512]{1,0:T(8,128)(2,1)S(1)} %bitcast.8, bf16[3328,512]{1,0:T(8,128)(2,1)} %features.3), custom_call_target="tpu_custom_call" | custom-call | tf_op jit(solution)/shard_map/finish/pallas_call | solution.py:327
  (3 shorter events, 0.1 us)
Async XLA Ops:
  0.6 70.4 %copy-start = (bf16[512,64]{0,1:T(8,128)(2,1)S(1)}, bf16[512,64]{0,1:T(8,128)(2,1)}, u32[]{:S(2)}) copy-start(bf16[512,64]{0,1:T(8,128)(2,1)} %param.3) | copy-start | bytes 196612
  3.9 10.0 %collective-permute-start = (f32[576,128]{1,0:T(8,128)S(1)}, f32[576,128]{1,0:T(8,128)S(1)}, u32[]{:S(2)}, u32[]{:S(2)}) collective-permute-start(f32[576,128]{1,0:T(8,128)S(1)} %get-tuple-element.9), channel_id=1, source_target_pairs={{0,1},{1,0},{2,3},{3,2},{4,5},{5,4},{6,7},{7,6},{8,9},{9,8},{10,11... | collective-permute-start | bytes 884744 | tf_op jit(solution)/shard_map/ppermute | solution.py:359
  63.0 8.0 %collective-permute-start.1 = (f32[576,128]{1,0:T(8,128)S(1)}, f32[576,128]{1,0:T(8,128)S(1)}, u32[]{:S(2)}, u32[]{:S(2)}) collective-permute-start(f32[576,128]{1,0:T(8,128)S(1)} %bitcast.6), channel_id=1, source_target_pairs={{0,1},{1,0},{2,3},{3,2},{4,5},{5,4},{6,7},{7,6},{8,9},{9,8},{10,11... | collective-permute-start | bytes 884744 | tf_op jit(solution)/shard_map/ppermute | solution.py:359

commit v9 on v8

--- a/solution.py
+++ b/solution.py
@@ -360,7 +360,7 @@
 
 
 def sum_everywhere(keep, send):
-    slab, line = ("near", "gx"), "far"
+    slab, line = ("near", "gx"), ("low", "high")
     cells, length = lax.axis_size(slab), lax.axis_size(line)
     half = keep + swap(send)
     rows, width = half.shape
@@ -376,7 +376,7 @@
 
 
 def on_device(features, sketch):
-    scale = math.sqrt(features.shape[0] * lax.axis_size(("gx", "far", "near", "c")))
+    scale = math.sqrt(features.shape[0] * lax.axis_size(("gx", "high", "low", "near", "c")))
     mine, other = sum_everywhere(*local_gram(features, core_index))
     basis, left, codes = finish(mine, other, sketch.T, features, scale, core_index)
     return (basis.T, codes.T, left.T)
@@ -384,8 +384,8 @@
 
 def solution(mesh):
     rows, columns = mesh.devices.shape
-    mesh = Mesh(mesh.devices.reshape(rows, columns // 4, 2, 2), ("gx", "far", "near", "c"))
-    split = P(("gx", "far", "near", "c"), None)
+    mesh = Mesh(mesh.devices.reshape(rows, columns // 8, 2, 2, 2), ("gx", "high", "low", "near", "c"))
+    split = P(("gx", "high", "low", "near", "c"), None)
     return jax.shard_map(
         on_device,
         mesh=mesh,

time: 80.2 us -> 79.9 us (level)
  no operation moved by 1% of the time
where the time goes in v9:
time: 79.9 us; the launch traced here: 79.6 us
  blocking collectives  48.7 us (61%)
  starting transfers between devices  15.4 us (19%)
  Pallas kernels  12.1 us (15%)
  waiting for transfers between devices  2.37 us (3%)
    all_to_all x3, blocking collectives, exchange(): return lax.all_to_all(parts, axes, split_axis=0, concat_axis=0, tiled=True)  48.7 us
    ppermute x2, starting transfers between devices, swap(): return lax.ppermute(x, 'c', [(0, 1), (1, 0)])  15.4 us
    pallas_call x1, Pallas kernels, finish(): pl.pallas_call(functools.partial(finish_kernel, scale, plan, core_of), ou...  8.94 us
    pallas_call x1, Pallas kernels, local_gram(): pl.pallas_call(functools.partial(gram_kernel, plan, core_of), out_shape=(...  3.2 us
    ppermute x2, waiting for transfers between devices, swap(): return lax.ppermute(x, 'c', [(0, 1), (1, 0)])  2.37 us
  transfers between devices with their start and end apart: 2, of which 2 were waited for; matrix products, arithmetic and copies ran while one was open for 0% of the time, Pallas kernels for 0%

profile of v9, /device:TPU:1, one launch (start us, length us, event | category | flops | bytes accessed | tf_op | source)
XLA Modules:
  0.0 79.6 jit_solution(634947269030338755)
XLA Ops:
  0.6 0.0 copy-start
  0.6 3.2 %gram.1 = (f32[576,128]{1,0:T(8,128)S(1)}, f32[576,128]{1,0:T(8,128)S(1)}) custom-call(bf16[3328,512]{1,0:T(8,128)(2,1)} %features.3), custom_call_target="tpu_custom_call" | custom-call | flops 1744830464 | bytes 3407872 | tf_op jit(solution)/shard_map/gram/pallas_call | solution.py:109
  3.9 8.8 %collective-permute-start = (f32[576,128]{1,0:T(8,128)S(1)}, f32[576,128]{1,0:T(8,128)S(1)}, u32[]{:S(2)}, u32[]{:S(2)}) collective-permute-start(f32[576,128]{1,0:T(8,128)S(1)} %get-tuple-element.9), channel_id=1, source_target_pairs={{0,1},{1,0},{2,3},{3,2},{4,5},{5,4},{6,7},{7,6},{8,9},{9,8},{10,11... | collective-permute-start | bytes 884744 | tf_op jit(solution)/shard_map/ppermute | solution.py:359
  12.6 1.2 %collective-permute-done = f32[576,128]{1,0:T(8,128)S(1)} collective-permute-done((f32[576,128]{1,0:T(8,128)S(1)}, f32[576,128]{1,0:T(8,128)S(1)}, u32[]{:S(2)}, u32[]{:S(2)}) %collective-permute-start) | collective-permute-done | bytes 294944 | tf_op jit(solution)/shard_map/ppermute | solution.py:359
  13.9 11.6 %all_to_all.15 = f32[32,9,2,128]{3,2,1,0:T(2,128)S(1)} all-to-all(f32[32,9,2,128]{3,2,1,0:T(2,128)S(1)} %bitcast.9), channel_id=1, replica_groups=mesh['gx'=16,'high'=4,'low'=2,'near'=2,'c'=2] {'near','gx'}, dimensions={0} | all-to-all | bytes 589824 | tf_op jit(solution)/shard_map/all_to_all | solution.py:355
  25.4 0.1 reduce_sum.18
  25.6 24.9 %all_to_all.16 = f32[8,9,2,128]{3,2,1,0:T(2,128)S(1)} all-to-all(f32[8,9,2,128]{3,2,1,0:T(2,128)S(1)} %broadcast_in_dim.6), channel_id=1, replica_groups=mesh['gx'=16,'high'=4,'low'=2,'near'=2,'c'=2] {'low','high'}, dimensions={0} | all-to-all | bytes 147456 | tf_op jit(solution)/shard_map/all_to_all | solution.py:355
  50.5 0.1 broadcast_in_dim.7
  50.6 12.3 %all_to_all.17 = f32[32,9,2,128]{3,2,1,0:T(2,128)S(1)} all-to-all(f32[32,9,2,128]{3,2,1,0:T(2,128)S(1)} %broadcast_in_dim.7), channel_id=1, replica_groups=mesh['gx'=16,'high'=4,'low'=2,'near'=2,'c'=2] {'near','gx'}, dimensions={0} | all-to-all | bytes 589824 | tf_op jit(solution)/shard_map/all_to_all | solution.py:355
  62.8 6.6 %collective-permute-start.1 = (f32[576,128]{1,0:T(8,128)S(1)}, f32[576,128]{1,0:T(8,128)S(1)}, u32[]{:S(2)}, u32[]{:S(2)}) collective-permute-start(f32[576,128]{1,0:T(8,128)S(1)} %bitcast.6), channel_id=1, source_target_pairs={{0,1},{1,0},{2,3},{3,2},{4,5},{5,4},{6,7},{7,6},{8,9},{9,8},{10,11... | collective-permute-start | bytes 884744 | tf_op jit(solution)/shard_map/ppermute | solution.py:359
  69.5 1.2 %collective-permute-done.1.other = f32[576,128]{1,0:T(8,128)S(1)} collective-permute-done((f32[576,128]{1,0:T(8,128)S(1)}, f32[576,128]{1,0:T(8,128)S(1)}, u32[]{:S(2)}, u32[]{:S(2)}) %collective-permute-start.1) | collective-permute-done | bytes 294944 | tf_op jit(solution)/shard_map/ppermute | solution.py:359
  70.7 0.0 copy-done
  70.7 8.9 %finish.1 = (f32[64,512]{1,0:T(8,128)}, f32[64,3328]{1,0:T(8,128)}, bf16[64,3328]{1,0:T(8,128)(2,1)}) custom-call(f32[576,128]{1,0:T(8,128)S(1)} %bitcast.7, f32[576,128]{1,0:T(8,128)S(1)} %collective-permute-done.1.other, bf16[64,512]{1,0:T(8,128)(2,1)S(1)} %bitcast.8, bf16[3328,512]{1,0:T(8,128)(2,1)} %features.3), custom_call_target="tpu_custom_call" | custom-call | tf_op jit(solution)/shard_map/finish/pallas_call | solution.py:327
  (3 shorter events, 0.1 us)
Async XLA Ops:
  0.6 70.1 %copy-start = (bf16[512,64]{0,1:T(8,128)(2,1)S(1)}, bf16[512,64]{0,1:T(8,128)(2,1)}, u32[]{:S(2)}) copy-start(bf16[512,64]{0,1:T(8,128)(2,1)} %param.3) | copy-start | bytes 196612
  3.9 10.0 %collective-permute-start = (f32[576,128]{1,0:T(8,128)S(1)}, f32[576,128]{1,0:T(8,128)S(1)}, u32[]{:S(2)}, u32[]{:S(2)}) collective-permute-start(f32[576,128]{1,0:T(8,128)S(1)} %get-tuple-element.9), channel_id=1, source_target_pairs={{0,1},{1,0},{2,3},{3,2},{4,5},{5,4},{6,7},{7,6},{8,9},{9,8},{10,11... | collective-permute-start | bytes 884744 | tf_op jit(solution)/shard_map/ppermute | solution.py:359
  62.8 7.8 %collective-permute-start.1 = (f32[576,128]{1,0:T(8,128)S(1)}, f32[576,128]{1,0:T(8,128)S(1)}, u32[]{:S(2)}, u32[]{:S(2)}) collective-permute-start(f32[576,128]{1,0:T(8,128)S(1)} %bitcast.6), channel_id=1, source_target_pairs={{0,1},{1,0},{2,3},{3,2},{4,5},{5,4},{6,7},{7,6},{8,9},{9,8},{10,11... | collective-permute-start | bytes 884744 | tf_op jit(solution)/shard_map/ppermute | solution.py:359
